TPU v7x, 32 devices: a whole 2x2x4 slice. The times are simulated.
32 devices in a mesh: ta: 8 (over z, x), gz: 2 (over y), gy: 2 (over core).
Axes of the slice: x: 2, y: 2, z: 4, core: 2. Of those that a mesh axis runs over, the one named last changes fastest.
Arguments:
- source_field: bfloat16 [8, 4, 4, 2, 256, 128], P('ta', 'gz', 'gy'), may hold values from -6 to 6
- clover: bfloat16 [8, 4, 4, 2, 128, 128], P('ta', 'gz', 'gy'), may hold values from -0.1875 to 0.1875
- forward: bfloat16 [4, 8, 4, 4, 2, 128, 128], P(None, 'ta', 'gz', 'gy'), may hold values from -0.1875 to 0.1875
- backward: bfloat16 [4, 8, 4, 4, 2, 128, 128], P(None, 'ta', 'gz', 'gy'), may hold values from -0.1875 to 0.1875
- restrict_blocks: bfloat16 [8, 4, 4, 2, 128, 128], P('ta', 'gz', 'gy'), may hold values from -0.1875 to 0.1875
Outputs:
- second_image: bfloat16 [8, 4, 4, 2, 256, 128], P('ta', 'gz', 'gy')
- restricted: bfloat16 [8, 4, 256, 128], P('ta')
All inputs are finite; a program needn't handle non-finite values.
Results may differ from a plain program's by a relative error of at most 0.0064.
Values may be sent and summed in bfloat16 or wider, within the bound.
A program may use at most 64 MiB of HBM per device.

v0:
```python
import jax
import jax.numpy as jnp
from jax import lax
from jax.sharding import PartitionSpec as P


def padded_2(block, sides, width):
    for axis, dim in sides:
        count = lax.axis_size(axis)
        forward = [(i, i + 1) for i in range(count - 1)]
        forward.append((count - 1, 0))
        backward = [(target, source) for source, target in forward]
        low = lax.ppermute(
            lax.slice_in_dim(block, block.shape[dim] - width, None, axis=dim), axis, forward
        )
        high = lax.ppermute(lax.slice_in_dim(block, 0, width, axis=dim), axis, backward)
        block = jnp.concatenate([low, block, high], axis=dim)
    return block


def shifted(block, axis, distance):
    devices = range(lax.axis_size(axis))
    route = [((i - distance) % len(devices), i) for i in devices]
    return lax.ppermute(block, axis, route)


def apply_block(blocks, vector):
    return jnp.einsum("tzyxij,tzyxrj->tzyxri", blocks, vector, preferred_element_type=jnp.float32)


def settle(formed):
    return lax.optimization_barrier(formed).astype(jnp.float32)


def operate_raw(vector, clover, forward, backward, shifted_blocks):
    padded = padded_2(vector, (("ta", 0), ("gz", 1), ("gy", 2)), 1)
    total = apply_block(clover, vector)
    total = total + apply_block(forward[0], padded[2:, 1:-1, 1:-1])
    total = total + apply_block(forward[1], padded[1:-1, 2:, 1:-1])
    total = total + apply_block(forward[2], padded[1:-1, 1:-1, 2:])
    total = total + apply_block(forward[3], jnp.roll(vector, -1, axis=3))
    total = total + settle(
        apply_block(shifted_blocks[0], padded[:-2, 1:-1, 1:-1]).astype(jnp.bfloat16)
    )
    total = total + settle(
        apply_block(shifted_blocks[1], padded[1:-1, :-2, 1:-1]).astype(jnp.bfloat16)
    )
    total = total + settle(
        apply_block(shifted_blocks[2], padded[1:-1, 1:-1, :-2]).astype(jnp.bfloat16)
    )
    formed_x = apply_block(backward[3], vector).astype(jnp.bfloat16)
    total = total + settle(jnp.roll(formed_x, 1, axis=3))
    return total.astype(jnp.bfloat16)


def per_device(source_field, clover, forward, backward, restrict_blocks):
    back_time = backward[0]
    back_zdir = backward[1]
    back_ydir = backward[2]
    shifted_time = jnp.concatenate([shifted(back_time, "ta", 1), back_time[:-1]], axis=0)
    shifted_zdir = jnp.concatenate([shifted(back_zdir[:, -1:], "gz", 1), back_zdir[:, :-1]], axis=1)
    shifted_ydir = jnp.concatenate(
        [shifted(back_ydir[:, :, -1:], "gy", 1), back_ydir[:, :, :-1]], axis=2
    )
    shifted_blocks = (shifted_time, shifted_zdir, shifted_ydir)
    first_image = operate_raw(source_field, clover, forward, backward, shifted_blocks)
    second_image = operate_raw(first_image, clover, forward, backward, shifted_blocks)
    partial_sum = jnp.einsum(
        "tzyxij,tzyxrj->ri", restrict_blocks, second_image, preferred_element_type=jnp.float32
    )
    own_part = partial_sum.astype(jnp.bfloat16).reshape(
        1, 1, partial_sum.shape[0], partial_sum.shape[1]
    )
    restricted = lax.all_gather(own_part, ("gz", "gy"), axis=1, tiled=True)
    return (second_image, restricted)


def solution(mesh):
    return jax.shard_map(
        per_device,
        mesh=mesh,
        in_specs=(
            P("ta", "gz", "gy", None, None, None),
            P("ta", "gz", "gy", None, None, None),
            P(None, "ta", "gz", "gy", None, None, None),
            P(None, "ta", "gz", "gy", None, None, None),
            P("ta", "gz", "gy", None, None, None),
        ),
        out_specs=(P("ta", "gz", "gy", None, None, None), P("ta", None, None, None)),
        check_vma=False,
    )
```

profile of v0, /device:TPU:0, one launch (start us, length us, event | category | flops | bytes accessed | tf_op | source)
XLA Modules:
  0.0 149.6 jit_solution(5764808749922863230)
XLA Ops:
  0.6 3.0 %collective-permute-start.1 = (bf16[1,2,2,2,256,128]{5,4,3,2,1,0:T(8,128)(2,1)}, bf16[1,2,2,2,256,128]{5,4,3,2,1,0:T(8,128)(2,1)S(1)}, u32[]{:S(2)}, u32[]{:S(2)}) collective-permute-start(bf16[1,2,2,2,256,128]{5,4,3,2,1,0:T(8,128)(2,1)} %param.5), channel_id=1, source_target_pairs={{0,4},{4,8},{8,12},{12,16},{16,20},{20,24},{24,28},{28,0},{1,5},{5... | collective-permute-start | bytes 1572872 | tf_op jit(solution)/shard_map/ppermute | solution.py:13
  3.6 3.1 %collective-permute-start = (bf16[1,2,2,2,256,128]{5,4,3,2,1,0:T(8,128)(2,1)}, bf16[1,2,2,2,256,128]{5,4,3,2,1,0:T(8,128)(2,1)S(1)}, u32[]{:S(2)}, u32[]{:S(2)}) collective-permute-start(bf16[1,2,2,2,256,128]{5,4,3,2,1,0:T(8,128)(2,1)} %param.5), channel_id=1, source_target_pairs={{4,0},{8,4},{12,8},{16,12},{20,16},{24,20},{28,24},{0,28},{5,1},{9... | collective-permute-start | bytes 1572872 | tf_op jit(solution)/shard_map/ppermute | solution.py:16
  6.7 19.6 %collective-permute-done.1 = bf16[1,2,2,2,256,128]{5,4,3,2,1,0:T(8,128)(2,1)S(1)} collective-permute-done((bf16[1,2,2,2,256,128]{5,4,3,2,1,0:T(8,128)(2,1)}, bf16[1,2,2,2,256,128]{5,4,3,2,1,0:T(8,128)(2,1)S(1)}, u32[]{:S(2)}, u32[]{:S(2)}) %collective-permute-start.1) | collective-permute-done | bytes 524320 | tf_op jit(solution)/shard_map/ppermute | solution.py:13
  26.4 1.1 constant_dynamic-update-slice_fusion.1
  27.5 0.9 collective-permute-done
  28.7 1.6 %collective-permute-start.2 = (bf16[3,1,2,2,256,128]{5,4,3,2,1,0:T(8,128)(2,1)S(1)}, bf16[3,1,2,2,256,128]{5,4,3,2,1,0:T(8,128)(2,1)S(1)}, u32[]{:S(2)}, u32[]{:S(2)}) collective-permute-start(bf16[3,1,2,2,256,128]{5,4,3,2,1,0:T(8,128)(2,1)S(1)} %get-tuple-element.9), channel_id=1, source_target_pairs={{2,0},{0,2},{3,1},{1,3},{6,4},{4,6},{7,5},{5,7},{10,8},{8,10},{11,... | collective-permute-start | bytes 2359304 | tf_op jit(solution)/shard_map/ppermute | solution.py:16
  30.3 0.5 collective-permute-start.3
  31.0 1.6 %collective-permute-start.6 = (bf16[1,1,2,2,128,128]{5,4,3,2,1,0:T(8,128)(2,1)S(1)}, bf16[1,1,2,2,128,128]{5,4,3,2,1,0:T(8,128)(2,1)S(1)}, u32[]{:S(2)}, u32[]{:S(2)}) collective-permute-start(bf16[1,1,2,2,128,128]{5,4,3,2,1,0:T(8,128)(2,1)S(1)} %get-tuple-element.21), channel_id=1, source_target_pairs={{2,0},{0,2},{3,1},{1,3},{6,4},{4,6},{7,5},{5,7},{10,8},{8,10},{11,... | collective-permute-start | bytes 393224 | tf_op jit(solution)/shard_map/ppermute | solution.py:24
  32.6 1.5 collective-permute-start.5
  34.1 0.3 fusion.19
  34.4 14.9 %collective-permute-done.2 = bf16[3,1,2,2,256,128]{5,4,3,2,1,0:T(8,128)(2,1)S(1)} collective-permute-done((bf16[3,1,2,2,256,128]{5,4,3,2,1,0:T(8,128)(2,1)S(1)}, bf16[3,1,2,2,256,128]{5,4,3,2,1,0:T(8,128)(2,1)S(1)}, u32[]{:S(2)}, u32[]{:S(2)}) %collective-permute-start.2) | collective-permute-done | bytes 786464 | tf_op jit(solution)/shard_map/ppermute | solution.py:16
  49.3 15.9 %collective-permute-done.3 = bf16[3,1,2,2,256,128]{5,4,3,2,1,0:T(8,128)(2,1)S(1)} collective-permute-done((bf16[3,1,2,2,256,128]{5,4,3,2,1,0:T(8,128)(2,1)S(1)}, bf16[3,1,2,2,256,128]{5,4,3,2,1,0:T(8,128)(2,1)S(1)}, u32[]{:S(2)}, u32[]{:S(2)}) %collective-permute-start.3) | collective-permute-done | bytes 786464 | tf_op jit(solution)/shard_map/ppermute | solution.py:13
  65.1 0.4 pad_maximum_fusion
  65.8 0.5 collective-permute-start.4
  66.5 0.6 copy-done.2
  67.1 0.3 fusion.51
  67.4 0.3 fusion.65
  67.7 0.3 convolution_add_fusion.3
  68.0 0.3 fusion.16
  68.3 0.3 fusion.17
  68.6 0.6 collective-permute-done.7
  69.2 0.3 fusion.18
  69.5 1.9 %collective-permute-done.4 = bf16[3,4,1,2,256,128]{5,4,3,2,1,0:T(8,128)(2,1)S(1)} collective-permute-done((bf16[3,4,1,2,256,128]{5,4,3,2,1,0:T(8,128)(2,1)S(1)}, bf16[3,4,1,2,256,128]{5,4,3,2,1,0:T(8,128)(2,1)S(1)}, u32[]{:S(2)}, u32[]{:S(2)}) %collective-permute-start.4) | collective-permute-done | bytes 1572896 | tf_op jit(solution)/shard_map/ppermute | solution.py:16
  71.5 0.3 fusion.45
  71.8 0.6 fusion.15
  72.4 1.8 %collective-permute-start.10 = (bf16[1,2,2,2,256,128]{5,4,3,2,1,0:T(8,128)(2,1)S(1)}, bf16[1,2,2,2,256,128]{5,4,3,2,1,0:T(8,128)(2,1)S(1)}, u32[]{:S(2)}, u32[]{:S(2)}) collective-permute-start(bf16[1,2,2,2,256,128]{5,4,3,2,1,0:T(8,128)(2,1)S(1)} %fusion.15), channel_id=1, source_target_pairs={{0,4},{4,8},{8,12},{12,16},{16,20},{20,24},{24,28},{28,0},{1,5},{5... | collective-permute-start | bytes 1572872 | tf_op jit(solution)/shard_map/ppermute | solution.py:13
  74.3 3.1 %collective-permute-start.9 = (bf16[1,2,2,2,256,128]{5,4,3,2,1,0:T(8,128)(2,1)S(1)}, bf16[1,2,2,2,256,128]{5,4,3,2,1,0:T(8,128)(2,1)S(1)}, u32[]{:S(2)}, u32[]{:S(2)}) collective-permute-start(bf16[1,2,2,2,256,128]{5,4,3,2,1,0:T(8,128)(2,1)S(1)} %fusion.15), channel_id=1, source_target_pairs={{4,0},{8,4},{12,8},{16,12},{20,16},{24,20},{28,24},{0,28},{5,1},{9... | collective-permute-start | bytes 1572872 | tf_op jit(solution)/shard_map/ppermute | solution.py:16
  77.4 19.6 %collective-permute-done.10 = bf16[1,2,2,2,256,128]{5,4,3,2,1,0:T(8,128)(2,1)S(1)} collective-permute-done((bf16[1,2,2,2,256,128]{5,4,3,2,1,0:T(8,128)(2,1)S(1)}, bf16[1,2,2,2,256,128]{5,4,3,2,1,0:T(8,128)(2,1)S(1)}, u32[]{:S(2)}, u32[]{:S(2)}) %collective-permute-start.10) | collective-permute-done | bytes 524320 | tf_op jit(solution)/shard_map/ppermute | solution.py:13
  97.0 2.3 %collective-permute-done.9 = bf16[1,2,2,2,256,128]{5,4,3,2,1,0:T(8,128)(2,1)S(1)} collective-permute-done((bf16[1,2,2,2,256,128]{5,4,3,2,1,0:T(8,128)(2,1)S(1)}, bf16[1,2,2,2,256,128]{5,4,3,2,1,0:T(8,128)(2,1)S(1)}, u32[]{:S(2)}, u32[]{:S(2)}) %collective-permute-start.9) | collective-permute-done | bytes 524320 | tf_op jit(solution)/shard_map/ppermute | solution.py:16
  99.6 1.6 %collective-permute-start.12 = (bf16[3,1,2,2,256,128]{5,4,3,2,1,0:T(8,128)(2,1)S(1)}, bf16[3,1,2,2,256,128]{5,4,3,2,1,0:T(8,128)(2,1)S(1)}, u32[]{:S(2)}, u32[]{:S(2)}) collective-permute-start(bf16[3,1,2,2,256,128]{5,4,3,2,1,0:T(8,128)(2,1)S(1)} %get-tuple-element.6), channel_id=1, source_target_pairs={{0,2},{2,0},{1,3},{3,1},{4,6},{6,4},{5,7},{7,5},{8,10},{10,8},{9,1... | collective-permute-start | bytes 2359304 | tf_op jit(solution)/shard_map/ppermute | solution.py:13
  101.2 0.5 collective-permute-start.11
  101.7 0.3 fusion.23
  102.0 18.1 %collective-permute-done.12 = bf16[3,1,2,2,256,128]{5,4,3,2,1,0:T(8,128)(2,1)S(1)} collective-permute-done((bf16[3,1,2,2,256,128]{5,4,3,2,1,0:T(8,128)(2,1)S(1)}, bf16[3,1,2,2,256,128]{5,4,3,2,1,0:T(8,128)(2,1)S(1)}, u32[]{:S(2)}, u32[]{:S(2)}) %collective-permute-start.12) | collective-permute-done | bytes 786464 | tf_op jit(solution)/shard_map/ppermute | solution.py:13
  120.2 14.9 %collective-permute-done.11 = bf16[3,1,2,2,256,128]{5,4,3,2,1,0:T(8,128)(2,1)S(1)} collective-permute-done((bf16[3,1,2,2,256,128]{5,4,3,2,1,0:T(8,128)(2,1)S(1)}, bf16[3,1,2,2,256,128]{5,4,3,2,1,0:T(8,128)(2,1)S(1)}, u32[]{:S(2)}, u32[]{:S(2)}) %collective-permute-start.11) | collective-permute-done | bytes 786464 | tf_op jit(solution)/shard_map/ppermute | solution.py:16
  135.1 0.4 pad_maximum_fusion.1
  135.9 0.5 collective-permute-start.13
  136.5 0.3 fusion.54
  136.8 0.3 fusion.60
  137.1 0.3 fusion.20
  137.4 0.3 convolution_add_fusion.1
  137.7 0.3 fusion.21
  138.0 1.2 collective-permute-done.14
  139.2 0.3 fusion.22
  139.6 1.9 %collective-permute-done.13 = bf16[3,4,1,2,256,128]{5,4,3,2,1,0:T(8,128)(2,1)S(1)} collective-permute-done((bf16[3,4,1,2,256,128]{5,4,3,2,1,0:T(8,128)(2,1)S(1)}, bf16[3,4,1,2,256,128]{5,4,3,2,1,0:T(8,128)(2,1)S(1)}, u32[]{:S(2)}, u32[]{:S(2)}) %collective-permute-start.13) | collective-permute-done | bytes 1572896 | tf_op jit(solution)/shard_map/ppermute | solution.py:16
  141.5 0.3 fusion.32
  141.8 0.7 fusion.14
  143.1 5.8 %all-gather = bf16[1024,128]{1,0:T(8,128)(2,1)S(1)} all-gather(bf16[256,128]{1,0:T(8,128)(2,1)S(1)} %fusion.24), channel_id=2, replica_groups=mesh['ta'=8,'gz'=2,'gy'=2] {'gz','gy'}, dimensions={0}, use_global_device_ids=true | all-gather | bytes 327680 | tf_op jit(solution)/shard_map/all_gather | solution.py:74
  148.9 0.7 copy.17
  (34 shorter events, 2.2 us)
Async XLA Ops:
  0.6 66.7 %copy-start = (bf16[1,2,2,2,128,128]{5,4,3,2,1,0:T(8,128)(2,1)S(1)}, bf16[1,2,2,2,128,128]{5,4,3,2,1,0:T(8,128)(2,1)}, u32[]{:S(2)}) copy-start(bf16[1,2,2,2,128,128]{5,4,3,2,1,0:T(8,128)(2,1)} %param.6) | copy-start | bytes 786436
  0.6 25.7 %collective-permute-start.1 = (bf16[1,2,2,2,256,128]{5,4,3,2,1,0:T(8,128)(2,1)}, bf16[1,2,2,2,256,128]{5,4,3,2,1,0:T(8,128)(2,1)S(1)}, u32[]{:S(2)}, u32[]{:S(2)}) collective-permute-start(bf16[1,2,2,2,256,128]{5,4,3,2,1,0:T(8,128)(2,1)} %param.5), channel_id=1, source_target_pairs={{0,4},{4,8},{8,12},{12,16},{16,20},{20,24},{24,28},{28,0},{1,5},{5... | collective-permute-start | bytes 1572872 | tf_op jit(solution)/shard_map/ppermute | solution.py:13
  3.6 24.8 %collective-permute-start = (bf16[1,2,2,2,256,128]{5,4,3,2,1,0:T(8,128)(2,1)}, bf16[1,2,2,2,256,128]{5,4,3,2,1,0:T(8,128)(2,1)S(1)}, u32[]{:S(2)}, u32[]{:S(2)}) collective-permute-start(bf16[1,2,2,2,256,128]{5,4,3,2,1,0:T(8,128)(2,1)} %param.5), channel_id=1, source_target_pairs={{4,0},{8,4},{12,8},{16,12},{20,16},{24,20},{28,24},{0,28},{5,1},{9... | collective-permute-start | bytes 1572872 | tf_op jit(solution)/shard_map/ppermute | solution.py:16
  28.5 2.3 %copy-start.3 = (bf16[4,1,2,2,2,128,128]{6,5,4,3,2,1,0:T(8,128)(2,1)S(1)}, bf16[4,1,2,2,2,128,128]{6,5,4,3,2,1,0:T(8,128)(2,1)}, u32[]{:S(2)}) copy-start(bf16[4,1,2,2,2,128,128]{6,5,4,3,2,1,0:T(8,128)(2,1)} %param.8) | copy-start | bytes 3145732
  28.7 5.4 %copy-start.1 = (bf16[1,2,2,2,256,128]{5,4,3,2,1,0:T(8,128)(2,1)S(1)}, bf16[1,2,2,2,256,128]{5,4,3,2,1,0:T(8,128)(2,1)}, u32[]{:S(2)}) copy-start(bf16[1,2,2,2,256,128]{5,4,3,2,1,0:T(8,128)(2,1)} %param.5) | copy-start | bytes 1572868
  28.7 20.5 %collective-permute-start.2 = (bf16[3,1,2,2,256,128]{5,4,3,2,1,0:T(8,128)(2,1)S(1)}, bf16[3,1,2,2,256,128]{5,4,3,2,1,0:T(8,128)(2,1)S(1)}, u32[]{:S(2)}, u32[]{:S(2)}) collective-permute-start(bf16[3,1,2,2,256,128]{5,4,3,2,1,0:T(8,128)(2,1)S(1)} %get-tuple-element.9), channel_id=1, source_target_pairs={{2,0},{0,2},{3,1},{1,3},{6,4},{4,6},{7,5},{5,7},{10,8},{8,10},{11,... | collective-permute-start | bytes 2359304 | tf_op jit(solution)/shard_map/ppermute | solution.py:16
  30.3 34.8 %collective-permute-start.3 = (bf16[3,1,2,2,256,128]{5,4,3,2,1,0:T(8,128)(2,1)S(1)}, bf16[3,1,2,2,256,128]{5,4,3,2,1,0:T(8,128)(2,1)S(1)}, u32[]{:S(2)}, u32[]{:S(2)}) collective-permute-start(bf16[3,1,2,2,256,128]{5,4,3,2,1,0:T(8,128)(2,1)S(1)} %get-tuple-element.8), channel_id=1, source_target_pairs={{0,2},{2,0},{1,3},{3,1},{4,6},{6,4},{5,7},{7,5},{8,10},{10,8},{9,1... | collective-permute-start | bytes 2359304 | tf_op jit(solution)/shard_map/ppermute | solution.py:13
  30.9 37.7 %collective-permute-start.8 = (bf16[1,2,1,2,128,128]{5,4,3,2,1,0:T(8,128)(2,1)S(1)}, bf16[1,2,1,2,128,128]{5,4,3,2,1,0:T(8,128)(2,1)S(1)}, u32[]{:S(2)}, u32[]{:S(2)}) collective-permute-start(bf16[1,2,1,2,128,128]{5,4,3,2,1,0:T(8,128)(2,1)S(1)} %get-tuple-element.23), channel_id=1, source_target_pairs={{1,0},{0,1},{3,2},{2,3},{5,4},{4,5},{7,6},{6,7},{9,8},{8,9},{11,10... | collective-permute-start | bytes 393224 | tf_op jit(solution)/shard_map/ppermute | solution.py:24
  31.0 37.3 %collective-permute-start.6 = (bf16[1,1,2,2,128,128]{5,4,3,2,1,0:T(8,128)(2,1)S(1)}, bf16[1,1,2,2,128,128]{5,4,3,2,1,0:T(8,128)(2,1)S(1)}, u32[]{:S(2)}, u32[]{:S(2)}) collective-permute-start(bf16[1,1,2,2,128,128]{5,4,3,2,1,0:T(8,128)(2,1)S(1)} %get-tuple-element.21), channel_id=1, source_target_pairs={{2,0},{0,2},{3,1},{1,3},{6,4},{4,6},{7,5},{5,7},{10,8},{8,10},{11,... | collective-permute-start | bytes 393224 | tf_op jit(solution)/shard_map/ppermute | solution.py:24
  32.6 35.4 %collective-permute-start.5 = (bf16[1,2,2,2,128,128]{5,4,3,2,1,0:T(8,128)(2,1)S(1)}, bf16[1,2,2,2,128,128]{5,4,3,2,1,0:T(8,128)(2,1)S(1)}, u32[]{:S(2)}, u32[]{:S(2)}) collective-permute-start(bf16[1,2,2,2,128,128]{5,4,3,2,1,0:T(8,128)(2,1)S(1)} %get-tuple-element.10), channel_id=1, source_target_pairs={{28,0},{0,4},{4,8},{8,12},{12,16},{16,20},{20,24},{24,28},{29,1},{... | collective-permute-start | bytes 786440 | tf_op jit(solution)/shard_map/ppermute | solution.py:24
  65.8 3.5 %collective-permute-start.7 = (bf16[3,4,1,2,256,128]{5,4,3,2,1,0:T(8,128)(2,1)S(1)}, bf16[3,4,1,2,256,128]{5,4,3,2,1,0:T(8,128)(2,1)S(1)}, u32[]{:S(2)}, u32[]{:S(2)}) collective-permute-start(bf16[3,4,1,2,256,128]{5,4,3,2,1,0:T(8,128)(2,1)S(1)} %get-tuple-element.4), channel_id=1, source_target_pairs={{0,1},{1,0},{2,3},{3,2},{4,5},{5,4},{6,7},{7,6},{8,9},{9,8},{10,11... | collective-permute-start | bytes 4718600 | tf_op jit(solution)/shard_map/ppermute | solution.py:13
  65.8 1.2 copy-start.2
  65.8 5.6 %collective-permute-start.4 = (bf16[3,4,1,2,256,128]{5,4,3,2,1,0:T(8,128)(2,1)S(1)}, bf16[3,4,1,2,256,128]{5,4,3,2,1,0:T(8,128)(2,1)S(1)}, u32[]{:S(2)}, u32[]{:S(2)}) collective-permute-start(bf16[3,4,1,2,256,128]{5,4,3,2,1,0:T(8,128)(2,1)S(1)} %get-tuple-element.5), channel_id=1, source_target_pairs={{1,0},{0,1},{3,2},{2,3},{5,4},{4,5},{7,6},{6,7},{9,8},{8,9},{11,10... | collective-permute-start | bytes 4718600 | tf_op jit(solution)/shard_map/ppermute | solution.py:16
  72.4 24.5 %collective-permute-start.10 = (bf16[1,2,2,2,256,128]{5,4,3,2,1,0:T(8,128)(2,1)S(1)}, bf16[1,2,2,2,256,128]{5,4,3,2,1,0:T(8,128)(2,1)S(1)}, u32[]{:S(2)}, u32[]{:S(2)}) collective-permute-start(bf16[1,2,2,2,256,128]{5,4,3,2,1,0:T(8,128)(2,1)S(1)} %fusion.15), channel_id=1, source_target_pairs={{0,4},{4,8},{8,12},{12,16},{16,20},{20,24},{24,28},{28,0},{1,5},{5... | collective-permute-start | bytes 1572872 | tf_op jit(solution)/shard_map/ppermute | solution.py:13
  74.3 25.0 %collective-permute-start.9 = (bf16[1,2,2,2,256,128]{5,4,3,2,1,0:T(8,128)(2,1)S(1)}, bf16[1,2,2,2,256,128]{5,4,3,2,1,0:T(8,128)(2,1)S(1)}, u32[]{:S(2)}, u32[]{:S(2)}) collective-permute-start(bf16[1,2,2,2,256,128]{5,4,3,2,1,0:T(8,128)(2,1)S(1)} %fusion.15), channel_id=1, source_target_pairs={{4,0},{8,4},{12,8},{16,12},{20,16},{24,20},{28,24},{0,28},{5,1},{9... | collective-permute-start | bytes 1572872 | tf_op jit(solution)/shard_map/ppermute | solution.py:16
  99.6 20.5 %collective-permute-start.12 = (bf16[3,1,2,2,256,128]{5,4,3,2,1,0:T(8,128)(2,1)S(1)}, bf16[3,1,2,2,256,128]{5,4,3,2,1,0:T(8,128)(2,1)S(1)}, u32[]{:S(2)}, u32[]{:S(2)}) collective-permute-start(bf16[3,1,2,2,256,128]{5,4,3,2,1,0:T(8,128)(2,1)S(1)} %get-tuple-element.6), channel_id=1, source_target_pairs={{0,2},{2,0},{1,3},{3,1},{4,6},{6,4},{5,7},{7,5},{8,10},{10,8},{9,1... | collective-permute-start | bytes 2359304 | tf_op jit(solution)/shard_map/ppermute | solution.py:13
  101.2 33.9 %collective-permute-start.11 = (bf16[3,1,2,2,256,128]{5,4,3,2,1,0:T(8,128)(2,1)S(1)}, bf16[3,1,2,2,256,128]{5,4,3,2,1,0:T(8,128)(2,1)S(1)}, u32[]{:S(2)}, u32[]{:S(2)}) collective-permute-start(bf16[3,1,2,2,256,128]{5,4,3,2,1,0:T(8,128)(2,1)S(1)} %get-tuple-element.7), channel_id=1, source_target_pairs={{2,0},{0,2},{3,1},{1,3},{6,4},{4,6},{7,5},{5,7},{10,8},{8,10},{11,... | collective-permute-start | bytes 2359304 | tf_op jit(solution)/shard_map/ppermute | solution.py:16
  135.8 3.5 %collective-permute-start.14 = (bf16[3,4,1,2,256,128]{5,4,3,2,1,0:T(8,128)(2,1)S(1)}, bf16[3,4,1,2,256,128]{5,4,3,2,1,0:T(8,128)(2,1)S(1)}, u32[]{:S(2)}, u32[]{:S(2)}) collective-permute-start(bf16[3,4,1,2,256,128]{5,4,3,2,1,0:T(8,128)(2,1)S(1)} %get-tuple-element.2), channel_id=1, source_target_pairs={{0,1},{1,0},{2,3},{3,2},{4,5},{5,4},{6,7},{7,6},{8,9},{9,8},{10,11... | collective-permute-start | bytes 4718600 | tf_op jit(solution)/shard_map/ppermute | solution.py:13
  135.9 5.6 %collective-permute-start.13 = (bf16[3,4,1,2,256,128]{5,4,3,2,1,0:T(8,128)(2,1)S(1)}, bf16[3,4,1,2,256,128]{5,4,3,2,1,0:T(8,128)(2,1)S(1)}, u32[]{:S(2)}, u32[]{:S(2)}) collective-permute-start(bf16[3,4,1,2,256,128]{5,4,3,2,1,0:T(8,128)(2,1)S(1)} %get-tuple-element.3), channel_id=1, source_target_pairs={{1,0},{0,1},{3,2},{2,3},{5,4},{4,5},{7,6},{6,7},{9,8},{8,9},{11,10... | collective-permute-start | bytes 4718600 | tf_op jit(solution)/shard_map/ppermute | solution.py:16
  141.8 1.0 copy-start.5
  142.8 6.8 %copy-start.4 = (bf16[1,2,2,2,256,128]{5,4,3,2,1,0:T(8,128)(2,1)}, bf16[1,2,2,2,256,128]{5,4,3,2,1,0:T(8,128)(2,1)S(1)}, u32[]{:S(2)}) copy-start(bf16[1,2,2,2,256,128]{5,4,3,2,1,0:T(8,128)(2,1)S(1)} %fusion.14) | copy-start | bytes 1572868
where the time goes:
time: 150 us
  waiting for transfers between devices  112 us (75%)
  starting transfers between devices  19.4 us (13%)
  matrix products  6.43 us (4%)
  blocking collectives  5.79 us (4%)
  local copies, waits for them, and re-layouts  3.78 us (3%)
    ppermute x6, waiting for transfers between devices, padded_2(): lax.ppermute(lax.slice_in_dim(block, block.shape[dim] - width, None, axis...  75.1 us
    ppermute x6, waiting for transfers between devices, padded_2(): lax.ppermute(lax.slice_in_dim(block, 0, width, axis=dim), axis, backward)  37 us
    ppermute x6, starting transfers between devices, padded_2(): lax.ppermute(lax.slice_in_dim(block, 0, width, axis=dim), axis, backward)  9.28 us
    ppermute x6, starting transfers between devices, padded_2(): lax.ppermute(lax.slice_in_dim(block, block.shape[dim] - width, None, axis...  7.05 us
    dot_general x18, matrix products, apply_block(): jnp.einsum('tzyxij,tzyxrj->tzyxri', blocks, vector, preferred_element_typ...  6.14 us
    all_gather x1, blocking collectives, per_device(): restricted = lax.all_gather(own_part, ('gz', 'gy'), axis=1, tiled=True)  5.79 us
    ppermute x3, starting transfers between devices, shifted(): return lax.ppermute(block, axis, route)  3.11 us
  transfers between devices with their start and end apart: 15, of which 12 were waited for; matrix products, arithmetic and copies ran while one was open for 4% of the time, Pallas kernels for 0%

commit v1 on v0

v1 whole, which is shorter than its diff:
```python
import functools

import jax
import jax.numpy as jnp
from jax import lax
from jax.experimental import pallas as pl
from jax.experimental.pallas import tpu as pltpu
from jax.sharding import PartitionSpec as P

MESH = pl.DeviceIdType.MESH
LAG = 2


def times(vector, block):
    return lax.dot_general(
        vector, block, (((1,), (1,)), ((), ())), preferred_element_type=jnp.float32
    )


def kernel(
    sizes,
    src, clo, fwd, bwd, res,
    image, gathered,
    V, T, PZ, PY, PX, B0, C, F, B, R, O, total_r, own_r,
    near_send, near_recv, far_send, far_recv, b0_send, b0_recv,
    z_send, z_recv, y_send, y_recv, local, out_sem, g_send, g_recv, g_local,
):
    n_ta, n_gz, n_gy = sizes
    ta, gz, gy = lax.axis_index("ta"), lax.axis_index("gz"), lax.axis_index("gy")
    odd = lax.rem(ta, 2)
    partner = ta + 1 - 2 * odd
    beyond = lax.rem(ta + 2 - 4 * odd + n_ta, n_ta)
    following = lax.rem(ta + 1, n_ta)
    z_up, z_down = lax.rem(gz + 1, n_gz), lax.rem(gz + n_gz - 1, n_gz)
    y_up, y_down = lax.rem(gy + 1, n_gy), lax.rem(gy + n_gy - 1, n_gy)

    fetch = [
        pltpu.make_async_copy(src, V.at[pl.ds(0, 8)], local.at[0]),
        pltpu.make_async_copy(bwd.at[pl.ds(8, 24)], B, local.at[1]),
        pltpu.make_async_copy(fwd, F, local.at[2]),
        pltpu.make_async_copy(clo, C, local.at[3]),
        pltpu.make_async_copy(res, R, local.at[4]),
    ]
    for copy in fetch:
        copy.start()

    others = [(a, b) for a in range(n_gz) for b in range(n_gy) if (a, b) != (0, 0)]

    def other(a, b):
        return lax.rem(gz + a, n_gz), lax.rem(gz * 0 + gy + b, n_gy)

    barrier = pltpu.get_barrier_semaphore()
    for step in (1, 2, n_ta - 1, n_ta - 2):
        pl.semaphore_signal(
            barrier, inc=1, device_id=(lax.rem(ta + step, n_ta), gz, gy), device_id_type=MESH
        )
    for a, b in others:
        oz, oy = other(a, b)
        pl.semaphore_signal(barrier, inc=1, device_id=(ta, oz, oy), device_id_type=MESH)
    pl.semaphore_wait(barrier, 4 + len(others))

    def remote(source, target, send, recv, device):
        return pltpu.make_async_remote_copy(
            src_ref=source, dst_ref=target, send_sem=send, recv_sem=recv,
            device_id=device, device_id_type=MESH,
        )

    def near(u, source):
        img, s = u // 8, lax.rem(u, 8)
        return remote(source, T.at[img, 1 - odd, s], near_send.at[u], near_recv.at[u],
                      (partner, gz, gy))

    def far(u):
        img, s = u // 8, lax.rem(u, 8)
        return remote(T.at[img, odd, s], T.at[img, 1 - odd, s], far_send.at[u], far_recv.at[u],
                      (beyond, gz, gy))

    def block0(s):
        return remote(bwd.at[s], B0.at[s], b0_send.at[s], b0_recv.at[s], (following, gz, gy))

    def z_vector(u, source):
        img, s = u // 8, lax.rem(u, 8)
        return remote(source, V.at[img * 16 + 8 + s], z_send.at[u], z_recv.at[u + 4],
                      (ta, z_down, gy))

    def z_formed(u):
        img, s = u // 8, lax.rem(u, 8)
        return remote(PZ.at[img * 12 + 4 + s], PZ.at[img * 12 + s - 4], z_send.at[u],
                      z_recv.at[u - 4], (ta, z_up, gy))

    def y_vector(u, source):
        img, s = u // 8, lax.rem(u, 8)
        k = 2 * (s // 4) + lax.rem(s, 2)
        return remote(source, V.at[img * 16 + 12 + k], y_send.at[u], y_recv.at[u + 2],
                      (ta, gz, y_down))

    def y_formed(u):
        img, s = u // 8, lax.rem(u, 8)
        k = 2 * (s // 4) + lax.rem(s, 2)
        return remote(PY.at[img * 12 + s], PY.at[img * 12 + 8 + k], y_send.at[u],
                      y_recv.at[u - 2], (ta, gz, y_up))

    def send_vector(u, source):
        s = lax.rem(u, 8)
        near(u, source).start()

        @pl.when(s < 4)
        def _():
            z_vector(u, source).start()

        @pl.when(lax.rem(s // 2, 2) == 0)
        def _():
            y_vector(u, source).start()

    def form(u):
        img, s = u // 8, lax.rem(u, 8)
        vector = V[img * 16 + s]
        PZ[img * 12 + 4 + s] = times(vector, B[s]).astype(jnp.bfloat16)

        @pl.when(s >= 4)
        def _():
            z_formed(u).start()

        PY[img * 12 + s] = times(vector, B[8 + s]).astype(jnp.bfloat16)

        @pl.when(lax.rem(s // 2, 2) == 1)
        def _():
            y_formed(u).start()

        PX[u] = times(vector, B[16 + s]).astype(jnp.bfloat16)

    @pl.loop(0, 8)
    def _(s):
        block0(s).start()
        send_vector(s, src.at[s])

    fetch[0].wait()
    fetch[1].wait()

    @pl.loop(0, 8)
    def _(s):
        form(s)

    for copy in fetch[2:]:
        copy.wait()
    total_r[...] = jnp.zeros_like(total_r)

    def finish(u):
        img, s = u // 8, lax.rem(u, 8)
        z, y, x = s // 4, lax.rem(s // 2, 2), lax.rem(s, 2)
        k = 2 * z + x
        base = img * 16
        y_next = base + (1 - y) * (s + 2) + y * (12 + k)
        y_from = img * 12 + y * (s - 2) + (1 - y) * (8 + k)
        flip = s + 1 - 2 * x

        @pl.when(u < 8)
        def _():
            block0(s).wait_recv()

        total = times(V[base + s], C[s]) + times(V[base + flip], F[24 + s])
        total = total + PX[img * 8 + flip].astype(jnp.float32)
        remote(V.at[base], V.at[base], z_send.at[u], z_recv.at[u], (ta, z_up, gy)).wait_recv()
        total = total + times(V[base + s + 4], F[8 + s])
        total = total + PZ[img * 12 + s].astype(jnp.float32)
        remote(V.at[base], V.at[base], y_send.at[u], y_recv.at[u], (ta, gz, y_up)).wait_recv()
        total = total + times(V[y_next], F[16 + s])
        total = total + PY[y_from].astype(jnp.float32)
        far(u).wait_recv()
        total = total + times(T[img, 0, s], F[s])
        total = total + times(T[img, 1, s], B0[s]).astype(jnp.bfloat16).astype(jnp.float32)
        value = total.astype(jnp.bfloat16)

        @pl.when(u < 8)
        def _():
            V[16 + s] = value
            send_vector(u + 8, V.at[16 + s])
            form(u + 8)

        @pl.when(u >= 8)
        def _():
            O[s] = value
            pltpu.make_async_copy(O.at[s], image.at[s], out_sem.at[s]).start()
            total_r[...] += times(value, R[s])

    @pl.loop(0, 16 + LAG)
    def _(u):
        @pl.when(u < 16)
        def _():
            near(u, V.at[0]).wait_recv()
            far(u).start()

        @pl.when(u >= LAG)
        def _():
            finish(u - LAG)

    own_r[...] = total_r[...].astype(jnp.bfloat16)
    place = gz * n_gy + gy
    sends = []
    for index, (a, b) in enumerate(others):
        oz, oy = other(a, b)
        copy = remote(own_r, gathered.at[place], g_send.at[index], g_recv.at[index], (ta, oz, oy))
        copy.start()
        sends.append(copy)
    keep = pltpu.make_async_copy(own_r, gathered.at[place], g_local)
    keep.start()

    @pl.loop(0, 16)
    def _(u):
        near(u, V.at[0]).wait_send()
        far(u).wait_send()
        remote(V.at[0], V.at[0], z_send.at[u], z_recv.at[u], (ta, z_up, gy)).wait_send()
        remote(V.at[0], V.at[0], y_send.at[u], y_recv.at[u], (ta, gz, y_up)).wait_send()

    @pl.loop(0, 8)
    def _(s):
        block0(s).wait_send()
        pltpu.make_async_copy(O.at[s], image.at[s], out_sem.at[s]).wait()

    keep.wait()
    for copy in sends:
        copy.wait()


def per_device(sizes, source_field, clover, forward, backward, restrict_blocks):
    n_ta, n_gz, n_gy = sizes
    rows, width = source_field.shape[-2:]
    field = (rows, width)
    block = (width, width)
    others = n_gz * n_gy - 1
    bf16 = jnp.bfloat16
    dma = pltpu.SemaphoreType.DMA
    image, gathered = pl.pallas_call(
        functools.partial(kernel, sizes),
        out_shape=(
            jax.ShapeDtypeStruct((8,) + field, bf16),
            jax.ShapeDtypeStruct((n_gz * n_gy,) + field, bf16),
        ),
        in_specs=[pl.BlockSpec(memory_space=pl.ANY)] * 5,
        out_specs=(pl.BlockSpec(memory_space=pl.ANY), pl.BlockSpec(memory_space=pl.ANY)),
        scratch_shapes=[
            pltpu.VMEM((32,) + field, bf16),
            pltpu.VMEM((2, 2, 8) + field, bf16),
            pltpu.VMEM((24,) + field, bf16),
            pltpu.VMEM((24,) + field, bf16),
            pltpu.VMEM((16,) + field, bf16),
            pltpu.VMEM((8,) + block, bf16),
            pltpu.VMEM((8,) + block, bf16),
            pltpu.VMEM((32,) + block, bf16),
            pltpu.VMEM((24,) + block, bf16),
            pltpu.VMEM((8,) + block, bf16),
            pltpu.VMEM((8,) + field, bf16),
            pltpu.VMEM(field, jnp.float32),
            pltpu.VMEM(field, bf16),
            dma((16,)), dma((16,)), dma((16,)), dma((16,)),
            dma((8,)), dma((8,)),
            dma((16,)), dma((16,)), dma((16,)), dma((16,)),
            dma((5,)), dma((8,)), dma((others,)), dma((others,)), dma,
        ],
        compiler_params=pltpu.CompilerParams(
            collective_id=0, has_side_effects=True, vmem_limit_bytes=40 * 1024 * 1024
        ),
    )(
        source_field.reshape((8,) + field),
        clover.reshape((8,) + block),
        forward.reshape((32,) + block),
        backward.reshape((32,) + block),
        restrict_blocks.reshape((8,) + block),
    )
    return image.reshape(source_field.shape), gathered.reshape((1, n_gz * n_gy) + field)


def solution(mesh):
    sizes = tuple(mesh.shape[axis] for axis in ("ta", "gz", "gy"))
    assert sizes[0] % 2 == 0 and sizes[0] >= 4
    return jax.shard_map(
        functools.partial(per_device, sizes),
        mesh=mesh,
        in_specs=(
            P("ta", "gz", "gy", None, None, None),
            P("ta", "gz", "gy", None, None, None),
            P(None, "ta", "gz", "gy", None, None, None),
            P(None, "ta", "gz", "gy", None, None, None),
            P("ta", "gz", "gy", None, None, None),
        ),
        out_specs=(P("ta", "gz", "gy", None, None, None), P("ta", None, None, None)),
        check_vma=False,
    )
```

time: 150 us -> 54.2 us (0.36)
  waiting for transfers between devices: 112 us -> 0 us
  Pallas kernels: 0 us -> 46.3 us
  starting transfers between devices: 19.4 us -> 0 us
  matrix products: 6.43 us -> 0 us
  blocking collectives: 5.79 us -> 0 us
  local copies, waits for them, and re-layouts: 3.78 us -> 6.88 us
    ppermute x15 -> x0, waiting for transfers between devices: 112 us -> none  [the longest x6 75.1 us: padded_2(): lax.ppermute(lax.slice_in_dim(block, block.shape[dim] - width, None, axis...]
    pallas_call x0 -> x1, Pallas kernels: none -> 46.3 us  [per_device(): pl.pallas_call(functools.partial(kernel, sizes), out_shape=(jax.ShapeDtyp...]
    ppermute x15 -> x0, starting transfers between devices: 19.4 us -> none  [the longest x6 9.28 us: padded_2(): lax.ppermute(lax.slice_in_dim(block, 0, width, axis=dim), axis, backward)]
    dot_general x19 -> x0, matrix products: 6.43 us -> none  [the longest x18 6.14 us: apply_block(): jnp.einsum('tzyxij,tzyxrj->tzyxri', blocks, vector, preferred_element_typ...]
    all_gather x1 -> x0, blocking collectives: 5.79 us -> none  [per_device(): restricted = lax.all_gather(own_part, ('gz', 'gy'), axis=1, tiled=True)]
    unnamed x15 -> x12, local copies, waits for them, and re-layouts: 2.71 us -> 6.88 us
  transfers between devices with their start and end apart: 15 -> 0, of which waited for: 12 -> 0; matrix products, arithmetic and copies ran while one was open for 4% -> 0% of each run, Pallas kernels for 0% -> 0%
where the time goes in v1:
time: 54.2 us; the launch traced here: 53.9 us
  Pallas kernels  46.3 us (85%)
  local copies, waits for them, and re-layouts  6.88 us (13%)
  between operations  0.65 us (1%)
    pallas_call x1, Pallas kernels, per_device(): pl.pallas_call(functools.partial(kernel, sizes), out_shape=(jax.ShapeDtyp...  46.3 us
    unnamed x12, local copies, waits for them, and re-layouts  6.88 us

profile of v1, /device:TPU:0, one launch (start us, length us, event | category | flops | bytes accessed | tf_op | source)
XLA Modules:
  0.0 53.9 jit_solution(12700889983528361198)
XLA Ops:
  0.6 0.0 copy-start
  0.6 1.2 %copy-done = bf16[4,1,2,2,2,128,128]{6,5,4,3,2,1,0:T(8,128)(2,1)S(1)} copy-done((bf16[4,1,2,2,2,128,128]{6,5,4,3,2,1,0:T(8,128)(2,1)S(1)}, bf16[4,1,2,2,2,128,128]{6,5,4,3,2,1,0:T(8,128)(2,1)}, u32[]{:S(2)}) %copy-start) | copy-done | bytes 1048600
  1.9 0.0 copy-start.1
  1.9 1.2 %copy-done.1 = bf16[4,1,2,2,2,128,128]{6,5,4,3,2,1,0:T(8,128)(2,1)S(1)} copy-done((bf16[4,1,2,2,2,128,128]{6,5,4,3,2,1,0:T(8,128)(2,1)S(1)}, bf16[4,1,2,2,2,128,128]{6,5,4,3,2,1,0:T(8,128)(2,1)}, u32[]{:S(2)}) %copy-start.1) | copy-done | bytes 1048600
  3.1 0.0 copy-start.2
  3.1 1.0 %copy-done.2 = bf16[1,2,2,2,256,128]{5,4,3,2,1,0:T(8,128)(2,1)S(1)} copy-done((bf16[1,2,2,2,256,128]{5,4,3,2,1,0:T(8,128)(2,1)S(1)}, bf16[1,2,2,2,256,128]{5,4,3,2,1,0:T(8,128)(2,1)}, u32[]{:S(2)}) %copy-start.2) | copy-done | bytes 524312
  4.1 0.0 copy-start.3
  4.1 0.9 %copy-done.3 = bf16[1,2,2,2,128,128]{5,4,3,2,1,0:T(8,128)(2,1)S(1)} copy-done((bf16[1,2,2,2,128,128]{5,4,3,2,1,0:T(8,128)(2,1)S(1)}, bf16[1,2,2,2,128,128]{5,4,3,2,1,0:T(8,128)(2,1)}, u32[]{:S(2)}) %copy-start.3) | copy-done | bytes 262168
  5.1 0.0 copy-start.4
  5.1 0.9 %copy-done.4 = bf16[1,2,2,2,128,128]{5,4,3,2,1,0:T(8,128)(2,1)S(1)} copy-done((bf16[1,2,2,2,128,128]{5,4,3,2,1,0:T(8,128)(2,1)S(1)}, bf16[1,2,2,2,128,128]{5,4,3,2,1,0:T(8,128)(2,1)}, u32[]{:S(2)}) %copy-start.4) | copy-done | bytes 262168
  6.0 46.3 %shard_map.68 = (bf16[8,256,128]{2,1,0:T(8,128)(2,1)S(1)}, bf16[4,256,128]{2,1,0:T(8,128)(2,1)S(1)}) custom-call(bf16[8,256,128]{2,1,0:T(8,128)(2,1)S(1)} %bitcast.10, bf16[8,128,128]{2,1,0:T(8,128)(2,1)S(1)} %bitcast.11, bf16[32,128,128]{2,1,0:T(8,128)(2,1)S(1)} %bitcast.7, bf16[32,128,128]{2,1,0:T(8,128)(2,1)S(1)} %bitcast.8, bf16[8,128,128]{2,1,0:T(8,128)(2,1)S(1)} %bitcast.12), custom_call_target="tpu_custom_call" | custom-call | tf_op jit(solution)/shard_map/pallas_call | solution.py:233
  52.4 0.8 %copy.9 = bf16[1,2,2,2,256,128]{5,4,3,2,1,0:T(8,128)(2,1)} copy(bf16[1,2,2,2,256,128]{5,4,3,2,1,0:T(8,128)(2,1)S(1)} %bitcast.9) | data formatting | bytes 1048576
  53.2 0.7 %copy.10 = bf16[1,4,256,128]{3,2,1,0:T(8,128)(2,1)} copy(bf16[1,4,256,128]{3,2,1,0:T(8,128)(2,1)S(1)} %bitcast.13) | data formatting | bytes 524288
Async XLA Ops:
  0.6 1.2 %copy-start = (bf16[4,1,2,2,2,128,128]{6,5,4,3,2,1,0:T(8,128)(2,1)S(1)}, bf16[4,1,2,2,2,128,128]{6,5,4,3,2,1,0:T(8,128)(2,1)}, u32[]{:S(2)}) copy-start(bf16[4,1,2,2,2,128,128]{6,5,4,3,2,1,0:T(8,128)(2,1)} %param.7) | copy-start | bytes 3145732
  1.9 1.2 %copy-start.1 = (bf16[4,1,2,2,2,128,128]{6,5,4,3,2,1,0:T(8,128)(2,1)S(1)}, bf16[4,1,2,2,2,128,128]{6,5,4,3,2,1,0:T(8,128)(2,1)}, u32[]{:S(2)}) copy-start(bf16[4,1,2,2,2,128,128]{6,5,4,3,2,1,0:T(8,128)(2,1)} %param.8) | copy-start | bytes 3145732
  3.1 1.0 %copy-start.2 = (bf16[1,2,2,2,256,128]{5,4,3,2,1,0:T(8,128)(2,1)S(1)}, bf16[1,2,2,2,256,128]{5,4,3,2,1,0:T(8,128)(2,1)}, u32[]{:S(2)}) copy-start(bf16[1,2,2,2,256,128]{5,4,3,2,1,0:T(8,128)(2,1)} %param.5) | copy-start | bytes 1572868
  4.1 0.9 %copy-start.3 = (bf16[1,2,2,2,128,128]{5,4,3,2,1,0:T(8,128)(2,1)S(1)}, bf16[1,2,2,2,128,128]{5,4,3,2,1,0:T(8,128)(2,1)}, u32[]{:S(2)}) copy-start(bf16[1,2,2,2,128,128]{5,4,3,2,1,0:T(8,128)(2,1)} %param.6) | copy-start | bytes 786436
  5.1 0.9 %copy-start.4 = (bf16[1,2,2,2,128,128]{5,4,3,2,1,0:T(8,128)(2,1)S(1)}, bf16[1,2,2,2,128,128]{5,4,3,2,1,0:T(8,128)(2,1)}, u32[]{:S(2)}) copy-start(bf16[1,2,2,2,128,128]{5,4,3,2,1,0:T(8,128)(2,1)} %param.9) | copy-start | bytes 786436

commit v2 on v1

--- a/solution.py
+++ b/solution.py
@@ -9,6 +9,7 @@
 
 MESH = pl.DeviceIdType.MESH
 LAG = 2
+AHEAD = 3
 
 
 def times(vector, block):
@@ -100,13 +101,26 @@
         return remote(PY.at[img * 12 + s], PY.at[img * 12 + 8 + k], y_send.at[u],
                       y_recv.at[u - 2], (ta, gz, y_up))
 
+    def send_time(u, source):
+        near(u, source).start()
+
+        @pl.when(u < 8)
+        def _():
+            block0(lax.rem(u, 8)).start()
+
+    def send_z(target):
+        img, d = target // 8, lax.rem(target, 8)
+
+        @pl.when(d < 4)
+        def _():
+            z_formed(target + 4).start()
+
+        @pl.when(d >= 4)
+        def _():
+            z_vector(target - 4, V.at[img * 16 + d - 4]).start()
+
     def send_vector(u, source):
         s = lax.rem(u, 8)
-        near(u, source).start()
-
-        @pl.when(s < 4)
-        def _():
-            z_vector(u, source).start()
 
         @pl.when(lax.rem(s // 2, 2) == 0)
         def _():
@@ -116,11 +130,6 @@
         img, s = u // 8, lax.rem(u, 8)
         vector = V[img * 16 + s]
         PZ[img * 12 + 4 + s] = times(vector, B[s]).astype(jnp.bfloat16)
-
-        @pl.when(s >= 4)
-        def _():
-            z_formed(u).start()
-
         PY[img * 12 + s] = times(vector, B[8 + s]).astype(jnp.bfloat16)
 
         @pl.when(lax.rem(s // 2, 2) == 1)
@@ -131,7 +140,10 @@
 
     @pl.loop(0, 8)
     def _(s):
-        block0(s).start()
+        @pl.when(s < AHEAD)
+        def _():
+            send_time(s, src.at[s])
+
         send_vector(s, src.at[s])
 
     fetch[0].wait()
@@ -139,7 +151,11 @@
 
     @pl.loop(0, 8)
     def _(s):
-        form(s)
+        form(lax.rem(s + 4, 8))
+
+        @pl.when(s < 4)
+        def _():
+            send_z(s)
 
     for copy in fetch[2:]:
         copy.wait()
@@ -183,12 +199,21 @@
             pltpu.make_async_copy(O.at[s], image.at[s], out_sem.at[s]).start()
             total_r[...] += times(value, R[s])
 
+        @pl.when(u < 12)
+        def _():
+            send_z(u + 4)
+
     @pl.loop(0, 16 + LAG)
     def _(u):
         @pl.when(u < 16)
         def _():
             near(u, V.at[0]).wait_recv()
             far(u).start()
+
+        @pl.when(u + AHEAD < 16)
+        def _():
+            v = u + AHEAD
+            send_time(v, V.at[v // 8 * 16 + lax.rem(v, 8)])
 
         @pl.when(u >= LAG)
         def _():
@@ -236,8 +261,8 @@
             jax.ShapeDtypeStruct((8,) + field, bf16),
             jax.ShapeDtypeStruct((n_gz * n_gy,) + field, bf16),
         ),
-        in_specs=[pl.BlockSpec(memory_space=pl.ANY)] * 5,
-        out_specs=(pl.BlockSpec(memory_space=pl.ANY), pl.BlockSpec(memory_space=pl.ANY)),
+        in_specs=[pl.BlockSpec(memory_space=pltpu.HBM)] * 5,
+        out_specs=(pl.BlockSpec(memory_space=pltpu.HBM), pl.BlockSpec(memory_space=pltpu.HBM)),
         scratch_shapes=[
             pltpu.VMEM((32,) + field, bf16),
             pltpu.VMEM((2, 2, 8) + field, bf16),
@@ -258,7 +283,7 @@
             dma((5,)), dma((8,)), dma((others,)), dma((others,)), dma,
         ],
         compiler_params=pltpu.CompilerParams(
-            collective_id=0, has_side_effects=True, vmem_limit_bytes=40 * 1024 * 1024
+            collective_id=0, has_side_effects=True, vmem_limit_bytes=60 * 1024 * 1024
         ),
     )(
         source_field.reshape((8,) + field),

time: 54.2 us -> 50.3 us (0.928)
  local copies, waits for them, and re-layouts: 6.88 us -> 2.62 us
    unnamed x12 -> x4, local copies, waits for them, and re-layouts: 6.88 us -> 2.62 us
where the time goes in v2:
time: 50.3 us; the launch traced here: 50.1 us
  Pallas kernels  46.8 us (93%)
  local copies, waits for them, and re-layouts  2.62 us (5%)
  between operations  0.65 us (1%)
    pallas_call x1, Pallas kernels, per_device(): pl.pallas_call(functools.partial(kernel, sizes), out_shape=(jax.ShapeDtyp...  46.8 us
    unnamed x4, local copies, waits for them, and re-layouts  2.62 us

profile of v2, /device:TPU:0, one launch (start us, length us, event | category | flops | bytes accessed | tf_op | source)
XLA Modules:
  0.0 50.1 jit_solution(8679488806767233781)
XLA Ops:
  0.6 46.8 %shard_map.68 = (bf16[8,256,128]{2,1,0:T(8,128)(2,1)}, bf16[4,256,128]{2,1,0:T(8,128)(2,1)}) custom-call(bf16[8,256,128]{2,1,0:T(8,128)(2,1)} %bitcast.10, bf16[8,128,128]{2,1,0:T(8,128)(2,1)} %bitcast.11, bf16[32,128,128]{2,1,0:T(8,128)(2,1)} %bitcast.7, bf16[32,128,128]{2,1,0:T(8,128)(2,1)} %bitcast.8, bf16[8,128,128]{2,1,0:T(8,128)(2,1)} %bitcast.12), custom_call_target="tpu_custom_call" | custom-call | tf_op jit(solution)/shard_map/pallas_call | solution.py:258
  47.4 0.0 copy-start
  47.4 1.9 %copy.9 = bf16[1,2,2,2,256,128]{5,4,3,2,1,0:T(8,128)(2,1)} copy(bf16[1,2,2,2,256,128]{5,4,3,2,1,0:T(8,128)(2,1)} %bitcast.9) | data formatting | bytes 1048576
  49.4 0.0 copy-done
  49.4 0.7 %copy.10 = bf16[1,4,256,128]{3,2,1,0:T(8,128)(2,1)} copy(bf16[1,4,256,128]{3,2,1,0:T(8,128)(2,1)S(1)} %bitcast.13) | data formatting | bytes 524288
Async XLA Ops:
  47.4 1.9 %copy-start = (bf16[4,256,128]{2,1,0:T(8,128)(2,1)S(1)}, bf16[4,256,128]{2,1,0:T(8,128)(2,1)}, u32[]{:S(2)}) copy-start(bf16[4,256,128]{2,1,0:T(8,128)(2,1)} %get-tuple-element.5) | copy-start | bytes 786436

commit v3 on v2

v3 whole, which is shorter than its diff:
```python
import functools

import jax
import jax.numpy as jnp
from jax import lax
from jax.experimental import pallas as pl
from jax.experimental.pallas import tpu as pltpu
from jax.sharding import PartitionSpec as P

MESH = pl.DeviceIdType.MESH
LAG = 5
AHEAD = 6
Z_AHEAD = 8
PARTS = 2
IMAGE = 8 * PARTS
UNITS = 2 * IMAGE


def times(vector, block):
    return lax.dot_general(
        vector, block, (((1,), (1,)), ((), ())), preferred_element_type=jnp.float32
    )


def kernel(
    sizes,
    src, clo, fwd, bwd, res,
    image, gathered,
    V, T, PZ, PY, PX, B0, C, F, B, R, O, total_r, own_r,
    near_send, near_recv, far_send, far_recv, b0_send, b0_recv,
    z_send, z_recv, y_send, y_recv, local, out_sem, g_send, g_recv, g_local,
):
    n_ta, n_gz, n_gy = sizes
    ta, gz, gy = lax.axis_index("ta"), lax.axis_index("gz"), lax.axis_index("gy")
    odd = lax.rem(ta, 2)
    partner = ta + 1 - 2 * odd
    beyond = lax.rem(ta + 2 - 4 * odd + n_ta, n_ta)
    following = lax.rem(ta + 1, n_ta)
    z_up, z_down = lax.rem(gz + 1, n_gz), lax.rem(gz + n_gz - 1, n_gz)
    y_up, y_down = lax.rem(gy + 1, n_gy), lax.rem(gy + n_gy - 1, n_gy)

    fetch = [
        pltpu.make_async_copy(src, V.at[pl.ds(0, 8)], local.at[0]),
        pltpu.make_async_copy(bwd.at[pl.ds(8, 24)], B, local.at[1]),
        pltpu.make_async_copy(fwd, F, local.at[2]),
        pltpu.make_async_copy(clo, C, local.at[3]),
        pltpu.make_async_copy(res, R, local.at[4]),
    ]
    for copy in fetch:
        copy.start()

    others = [(a, b) for a in range(n_gz) for b in range(n_gy) if (a, b) != (0, 0)]

    def other(a, b):
        return lax.rem(gz + a, n_gz), lax.rem(gz * 0 + gy + b, n_gy)

    barrier = pltpu.get_barrier_semaphore()
    for step in (1, 2, n_ta - 1, n_ta - 2):
        pl.semaphore_signal(
            barrier, inc=1, device_id=(lax.rem(ta + step, n_ta), gz, gy), device_id_type=MESH
        )
    for a, b in others:
        oz, oy = other(a, b)
        pl.semaphore_signal(barrier, inc=1, device_id=(ta, oz, oy), device_id_type=MESH)
    pl.semaphore_wait(barrier, 4 + len(others))

    def remote(source, target, send, recv, device):
        return pltpu.make_async_remote_copy(
            src_ref=source, dst_ref=target, send_sem=send, recv_sem=recv,
            device_id=device, device_id_type=MESH,
        )

    rows = src.shape[1] // PARTS

    def split(u):
        part = lax.rem(u // 8, PARTS)
        return u // IMAGE, pl.ds(pl.multiple_of(part * rows, rows), rows), lax.rem(u, 8)

    def near(u, source):
        img, r, s = split(u)
        return remote(source.at[r], T.at[img, 1 - odd, s, r], near_send.at[u], near_recv.at[u],
                      (partner, gz, gy))

    def far(u):
        img, r, s = split(u)
        return remote(T.at[img, odd, s, r], T.at[img, 1 - odd, s, r], far_send.at[u],
                      far_recv.at[u], (beyond, gz, gy))

    def block0(s):
        return remote(bwd.at[s], B0.at[s], b0_send.at[s], b0_recv.at[s], (following, gz, gy))

    def z_vector(u):
        img, r, s = split(u)
        return remote(V.at[img * 16 + s, r], V.at[img * 16 + 8 + s, r], z_send.at[u],
                      z_recv.at[u + 4], (ta, z_down, gy))

    def z_formed(u):
        img, r, s = split(u)
        return remote(PZ.at[img * 12 + 4 + s, r], PZ.at[img * 12 + s - 4, r], z_send.at[u],
                      z_recv.at[u - 4], (ta, z_up, gy))

    def z_any(u):
        return remote(V.at[0, pl.ds(0, rows)], V.at[0, pl.ds(0, rows)], z_send.at[u],
                      z_recv.at[u], (ta, z_up, gy))

    def y_vector(u):
        img, r, s = split(u)
        k = 2 * (s // 4) + lax.rem(s, 2)
        return remote(V.at[img * 16 + s, r], V.at[img * 16 + 12 + k, r], y_send.at[u],
                      y_recv.at[u + 2], (ta, gz, y_down))

    def y_formed(u):
        img, r, s = split(u)
        k = 2 * (s // 4) + lax.rem(s, 2)
        return remote(PY.at[img * 12 + s, r], PY.at[img * 12 + 8 + k, r], y_send.at[u],
                      y_recv.at[u - 2], (ta, gz, y_up))

    def y_any(u):
        return remote(V.at[0, pl.ds(0, rows)], V.at[0, pl.ds(0, rows)], y_send.at[u],
                      y_recv.at[u], (ta, gz, y_up))

    def send_time(u, source):
        near(u, source).start()

        @pl.when(u < 8)
        def _():
            block0(lax.rem(u, 8)).start()

    def send_z(target):
        @pl.when(lax.rem(target, 8) < 4)
        def _():
            z_formed(target + 4).start()

        @pl.when(lax.rem(target, 8) >= 4)
        def _():
            z_vector(target - 4).start()

    def send_y(u):
        y = lax.rem(u // 2, 2)

        @pl.when(y == 0)
        def _():
            y_vector(u).start()

        @pl.when(y == 1)
        def _():
            y_formed(u).start()

    def form(img, r, s, vector):
        block = jnp.concatenate([B[s], B[8 + s], B[16 + s]], axis=0)
        formed = times(vector, block).astype(jnp.bfloat16)
        width = vector.shape[1]
        PZ[img * 12 + 4 + s, r] = formed[:, :width]
        PY[img * 12 + s, r] = formed[:, width : 2 * width]
        PX[img * 8 + s, r] = formed[:, 2 * width :]

    @pl.loop(0, AHEAD)
    def _(u):
        send_time(u, src.at[lax.rem(u, 8)])

    fetch[0].wait()
    fetch[1].wait()

    @pl.loop(0, 8)
    def _(index):
        s = lax.rem(index + 4, 8)
        everything = pl.ds(0, PARTS * rows)
        form(0, everything, s, V[s])

        @pl.when(index < 4)
        def _():
            send_z(index)

        send_y(s)

    @pl.loop(4, Z_AHEAD)
    def _(u):
        send_z(u)

    @pl.loop(8, IMAGE)
    def _(u):
        send_y(u)

    for copy in fetch[2:]:
        copy.wait()
    total_r[...] = jnp.zeros_like(total_r)

    place = gz * n_gy + gy

    def gather(part):
        r = pl.ds(pl.multiple_of(part * rows, rows), rows)
        copies = [pltpu.make_async_copy(own_r.at[r], gathered.at[place, r], g_local.at[part])]
        for index, (a, b) in enumerate(others):
            oz, oy = other(a, b)
            copies.append(remote(own_r.at[r], gathered.at[place, r], g_send.at[part, index],
                                 g_recv.at[part, index], (ta, oz, oy)))
        return copies

    def result(u):
        img, r, s = split(u)
        return pltpu.make_async_copy(O.at[s, r], image.at[s, r], out_sem.at[u - IMAGE])

    def finish(u):
        img, r, s = split(u)
        z, y, x = s // 4, lax.rem(s // 2, 2), lax.rem(s, 2)
        k = 2 * z + x
        base = img * 16
        y_next = base + (1 - y) * (s + 2) + y * (12 + k)
        y_from = img * 12 + y * (s - 2) + (1 - y) * (8 + k)
        flip = s + 1 - 2 * x

        @pl.when(u < 8)
        def _():
            block0(s).wait_recv()

        z_any(u).wait_recv()
        y_any(u).wait_recv()
        far(u).wait_recv()
        vectors = [V[base + s, r], V[base + flip, r], V[base + s + 4, r], V[y_next, r],
                   T[img, 0, s, r]]
        blocks = [C[s], F[24 + s], F[8 + s], F[16 + s], F[s]]
        total = times(jnp.concatenate(vectors, axis=1), jnp.concatenate(blocks, axis=1))
        for formed in (PX[img * 8 + flip, r], PZ[img * 12 + s, r], PY[y_from, r],
                       times(T[img, 1, s, r], B0[s]).astype(jnp.bfloat16)):
            total = total + formed.astype(jnp.float32)
        value = total.astype(jnp.bfloat16)

        @pl.when(u < IMAGE)
        def _():
            V[16 + s, r] = value
            form(1, r, s, value)
            send_y(u + IMAGE)

        @pl.when(u >= IMAGE)
        def _():
            O[s, r] = value
            result(u).start()
            total_r[r] += times(value, R[s])

            @pl.when(s == 7)
            def _():
                own_r[r] = total_r[r].astype(jnp.bfloat16)
                for copy in gather(lax.rem(u // 8, PARTS)):
                    copy.start()

        @pl.when(u + Z_AHEAD < UNITS)
        def _():
            send_z(u + Z_AHEAD)

    @pl.loop(0, UNITS + LAG)
    def _(u):
        @pl.when(u < UNITS)
        def _():
            near(u, V.at[0]).wait_recv()
            far(u).start()

        @pl.when(u + AHEAD < UNITS)
        def _():
            v = u + AHEAD
            send_time(v, V.at[v // IMAGE * 16 + lax.rem(v, 8)])

        @pl.when(u >= LAG)
        def _():
            finish(u - LAG)

    @pl.loop(0, UNITS)
    def _(u):
        near(u, V.at[0]).wait_send()
        far(u).wait_send()
        z_any(u).wait_send()
        y_any(u).wait_send()

    @pl.loop(0, 8)
    def _(s):
        block0(s).wait_send()

    @pl.loop(IMAGE, UNITS)
    def _(u):
        result(u).wait()

    @pl.loop(0, PARTS)
    def _(part):
        for copy in gather(part):
            copy.wait()


def per_device(sizes, source_field, clover, forward, backward, restrict_blocks):
    n_ta, n_gz, n_gy = sizes
    rows, width = source_field.shape[-2:]
    field = (rows, width)
    block = (width, width)
    others = n_gz * n_gy - 1
    bf16 = jnp.bfloat16
    dma = pltpu.SemaphoreType.DMA
    image, gathered = pl.pallas_call(
        functools.partial(kernel, sizes),
        out_shape=(
            jax.ShapeDtypeStruct((8,) + field, bf16),
            jax.ShapeDtypeStruct((n_gz * n_gy,) + field, bf16),
        ),
        in_specs=[pl.BlockSpec(memory_space=pltpu.HBM)] * 5,
        out_specs=(pl.BlockSpec(memory_space=pltpu.HBM), pl.BlockSpec(memory_space=pltpu.HBM)),
        scratch_shapes=[
            pltpu.VMEM((32,) + field, bf16),
            pltpu.VMEM((2, 2, 8) + field, bf16),
            pltpu.VMEM((24,) + field, bf16),
            pltpu.VMEM((24,) + field, bf16),
            pltpu.VMEM((16,) + field, bf16),
            pltpu.VMEM((8,) + block, bf16),
            pltpu.VMEM((8,) + block, bf16),
            pltpu.VMEM((32,) + block, bf16),
            pltpu.VMEM((24,) + block, bf16),
            pltpu.VMEM((8,) + block, bf16),
            pltpu.VMEM((8,) + field, bf16),
            pltpu.VMEM(field, jnp.float32),
            pltpu.VMEM(field, bf16),
            dma((UNITS,)), dma((UNITS,)), dma((UNITS,)), dma((UNITS,)),
            dma((8,)), dma((8,)),
            dma((UNITS,)), dma((UNITS,)), dma((UNITS,)), dma((UNITS,)),
            dma((5,)), dma((IMAGE,)), dma((PARTS, others)), dma((PARTS, others)), dma((PARTS,)),
        ],
        compiler_params=pltpu.CompilerParams(
            collective_id=0, has_side_effects=True, vmem_limit_bytes=60 * 1024 * 1024
        ),
    )(
        source_field.reshape((8,) + field),
        clover.reshape((8,) + block),
        forward.reshape((32,) + block),
        backward.reshape((32,) + block),
        restrict_blocks.reshape((8,) + block),
    )
    return image.reshape(source_field.shape), gathered.reshape((1, n_gz * n_gy) + field)


def solution(mesh):
    sizes = tuple(mesh.shape[axis] for axis in ("ta", "gz", "gy"))
    assert sizes[0] % 2 == 0 and sizes[0] >= 4
    return jax.shard_map(
        functools.partial(per_device, sizes),
        mesh=mesh,
        in_specs=(
            P("ta", "gz", "gy", None, None, None),
            P("ta", "gz", "gy", None, None, None),
            P(None, "ta", "gz", "gy", None, None, None),
            P(None, "ta", "gz", "gy", None, None, None),
            P("ta", "gz", "gy", None, None, None),
        ),
        out_specs=(P("ta", "gz", "gy", None, None, None), P("ta", None, None, None)),
        check_vma=False,
    )
```

time: 50.3 us -> 49.7 us (0.988)
  no operation moved by 1% of the time
where the time goes in v3:
time: 49.7 us; the launch traced here: 49.6 us
  Pallas kernels  46.3 us (93%)
  local copies, waits for them, and re-layouts  2.62 us (5%)
  between operations  0.65 us (1%)
    pallas_call x1, Pallas kernels, per_device(): pl.pallas_call(functools.partial(kernel, sizes), out_shape=(jax.ShapeDtyp...  46.3 us
    unnamed x4, local copies, waits for them, and re-layouts  2.62 us

profile of v3, /device:TPU:0, one launch (start us, length us, event | category | flops | bytes accessed | tf_op | source)
XLA Modules:
  0.0 49.6 jit_solution(16639059700885644905)
XLA Ops:
  0.6 46.3 %shard_map.68 = (bf16[8,256,128]{2,1,0:T(8,128)(2,1)}, bf16[4,256,128]{2,1,0:T(8,128)(2,1)}) custom-call(bf16[8,256,128]{2,1,0:T(8,128)(2,1)} %bitcast.10, bf16[8,128,128]{2,1,0:T(8,128)(2,1)} %bitcast.11, bf16[32,128,128]{2,1,0:T(8,128)(2,1)} %bitcast.7, bf16[32,128,128]{2,1,0:T(8,128)(2,1)} %bitcast.8, bf16[8,128,128]{2,1,0:T(8,128)(2,1)} %bitcast.12), custom_call_target="tpu_custom_call" | custom-call | tf_op jit(solution)/shard_map/pallas_call | solution.py:295
  46.9 0.0 copy-start
  47.0 1.9 %copy.9 = bf16[1,2,2,2,256,128]{5,4,3,2,1,0:T(8,128)(2,1)} copy(bf16[1,2,2,2,256,128]{5,4,3,2,1,0:T(8,128)(2,1)} %bitcast.9) | data formatting | bytes 1048576
  48.9 0.0 copy-done
  48.9 0.7 %copy.10 = bf16[1,4,256,128]{3,2,1,0:T(8,128)(2,1)} copy(bf16[1,4,256,128]{3,2,1,0:T(8,128)(2,1)S(1)} %bitcast.13) | data formatting | bytes 524288
Async XLA Ops:
  46.9 1.9 %copy-start = (bf16[4,256,128]{2,1,0:T(8,128)(2,1)S(1)}, bf16[4,256,128]{2,1,0:T(8,128)(2,1)}, u32[]{:S(2)}) copy-start(bf16[4,256,128]{2,1,0:T(8,128)(2,1)} %get-tuple-element.5) | copy-start | bytes 786436

commit v4 on v3

--- a/solution.py
+++ b/solution.py
@@ -8,7 +8,7 @@
 from jax.sharding import PartitionSpec as P
 
 MESH = pl.DeviceIdType.MESH
-LAG = 5
+LAG = 4
 AHEAD = 6
 Z_AHEAD = 8
 PARTS = 2
@@ -26,7 +26,7 @@
     sizes,
     src, clo, fwd, bwd, res,
     image, gathered,
-    V, T, PZ, PY, PX, B0, C, F, B, R, O, total_r, own_r,
+    V, T, PZ, PY, PX, TB, C, F, B, R, O, early, total_r, own_r,
     near_send, near_recv, far_send, far_recv, b0_send, b0_recv,
     z_send, z_recv, y_send, y_recv, local, out_sem, g_send, g_recv, g_local,
 ):
@@ -42,9 +42,10 @@
     fetch = [
         pltpu.make_async_copy(src, V.at[pl.ds(0, 8)], local.at[0]),
         pltpu.make_async_copy(bwd.at[pl.ds(8, 24)], B, local.at[1]),
-        pltpu.make_async_copy(fwd, F, local.at[2]),
+        pltpu.make_async_copy(fwd.at[pl.ds(8, 24)], F, local.at[2]),
         pltpu.make_async_copy(clo, C, local.at[3]),
         pltpu.make_async_copy(res, R, local.at[4]),
+        pltpu.make_async_copy(fwd.at[pl.ds(0, 8)], TB.at[0], local.at[5]),
     ]
     for copy in fetch:
         copy.start()
@@ -87,7 +88,7 @@
                       far_recv.at[u], (beyond, gz, gy))
 
     def block0(s):
-        return remote(bwd.at[s], B0.at[s], b0_send.at[s], b0_recv.at[s], (following, gz, gy))
+        return remote(bwd.at[s], TB.at[1, s], b0_send.at[s], b0_recv.at[s], (following, gz, gy))
 
     def z_vector(u):
         img, r, s = split(u)
@@ -200,7 +201,11 @@
         img, r, s = split(u)
         return pltpu.make_async_copy(O.at[s, r], image.at[s, r], out_sem.at[u - IMAGE])
 
-    def finish(u):
+    def time_term(img, slot, s, r):
+        term = times(T[img, slot, s, r], TB[slot, s])
+        return jnp.where(slot == 1, term.astype(jnp.bfloat16).astype(jnp.float32), term)
+
+    def begin(u):
         img, r, s = split(u)
         z, y, x = s // 4, lax.rem(s // 2, 2), lax.rem(s, 2)
         k = 2 * z + x
@@ -215,14 +220,18 @@
 
         z_any(u).wait_recv()
         y_any(u).wait_recv()
+        vectors = [V[base + s, r], V[base + flip, r], V[base + s + 4, r], V[y_next, r]]
+        blocks = [C[s], F[16 + s], F[s], F[8 + s]]
+        total = times(jnp.concatenate(vectors, axis=1), jnp.concatenate(blocks, axis=1))
+        total = total + time_term(img, odd, s, r)
+        for formed in (PX[img * 8 + flip, r], PZ[img * 12 + s, r], PY[y_from, r]):
+            total = total + formed.astype(jnp.float32)
+        early[lax.rem(u, 8)] = total
+
+    def finish(u):
+        img, r, s = split(u)
         far(u).wait_recv()
-        vectors = [V[base + s, r], V[base + flip, r], V[base + s + 4, r], V[y_next, r],
-                   T[img, 0, s, r]]
-        blocks = [C[s], F[24 + s], F[8 + s], F[16 + s], F[s]]
-        total = times(jnp.concatenate(vectors, axis=1), jnp.concatenate(blocks, axis=1))
-        for formed in (PX[img * 8 + flip, r], PZ[img * 12 + s, r], PY[y_from, r],
-                       times(T[img, 1, s, r], B0[s]).astype(jnp.bfloat16)):
-            total = total + formed.astype(jnp.float32)
+        total = early[lax.rem(u, 8)] + time_term(img, 1 - odd, s, r)
         value = total.astype(jnp.bfloat16)
 
         @pl.when(u < IMAGE)
@@ -259,6 +268,10 @@
             v = u + AHEAD
             send_time(v, V.at[v // IMAGE * 16 + lax.rem(v, 8)])
 
+        @pl.when(u < UNITS)
+        def _():
+            begin(u)
+
         @pl.when(u >= LAG)
         def _():
             finish(u - LAG)
@@ -282,6 +295,39 @@
     def _(part):
         for copy in gather(part):
             copy.wait()
+
+
+def write(image, gathered, image_out, gathered_out, held, inward, outward):
+    parts = [(image.at[s], image_out.at[s]) for s in range(image.shape[0])]
+    parts += [(gathered.at[s], gathered_out.at[s]) for s in range(gathered.shape[0])]
+    reads = [pltpu.make_async_copy(a, held.at[i], inward.at[i]) for i, (a, _) in enumerate(parts)]
+    writes = [pltpu.make_async_copy(held.at[i], b, outward.at[i]) for i, (_, b) in enumerate(parts)]
+    for copy in reads:
+        copy.start()
+    for read, copy in zip(reads, writes):
+        read.wait()
+        copy.start()
+    for copy in writes:
+        copy.wait()
+
+
+def written(image, gathered):
+    count = image.shape[0] + gathered.shape[0]
+    return pl.pallas_call(
+        write,
+        out_shape=(
+            jax.ShapeDtypeStruct(image.shape, image.dtype),
+            jax.ShapeDtypeStruct(gathered.shape, gathered.dtype),
+        ),
+        in_specs=[pl.BlockSpec(memory_space=pltpu.HBM)] * 2,
+        out_specs=(pl.BlockSpec(memory_space=pltpu.HBM), pl.BlockSpec(memory_space=pltpu.HBM)),
+        scratch_shapes=[
+            pltpu.VMEM((count,) + image.shape[1:], image.dtype),
+            pltpu.SemaphoreType.DMA((count,)),
+            pltpu.SemaphoreType.DMA((count,)),
+        ],
+        compiler_params=pltpu.CompilerParams(vmem_limit_bytes=60 * 1024 * 1024),
+    )(image, gathered)
 
 
 def per_device(sizes, source_field, clover, forward, backward, restrict_blocks):
@@ -306,18 +352,19 @@
             pltpu.VMEM((24,) + field, bf16),
             pltpu.VMEM((24,) + field, bf16),
             pltpu.VMEM((16,) + field, bf16),
+            pltpu.VMEM((2, 8) + block, bf16),
             pltpu.VMEM((8,) + block, bf16),
-            pltpu.VMEM((8,) + block, bf16),
-            pltpu.VMEM((32,) + block, bf16),
+            pltpu.VMEM((24,) + block, bf16),
             pltpu.VMEM((24,) + block, bf16),
             pltpu.VMEM((8,) + block, bf16),
             pltpu.VMEM((8,) + field, bf16),
+            pltpu.VMEM((8, rows // PARTS, width), jnp.float32),
             pltpu.VMEM(field, jnp.float32),
             pltpu.VMEM(field, bf16),
             dma((UNITS,)), dma((UNITS,)), dma((UNITS,)), dma((UNITS,)),
             dma((8,)), dma((8,)),
             dma((UNITS,)), dma((UNITS,)), dma((UNITS,)), dma((UNITS,)),
-            dma((5,)), dma((IMAGE,)), dma((PARTS, others)), dma((PARTS, others)), dma((PARTS,)),
+            dma((6,)), dma((IMAGE,)), dma((PARTS, others)), dma((PARTS, others)), dma((PARTS,)),
         ],
         compiler_params=pltpu.CompilerParams(
             collective_id=0, has_side_effects=True, vmem_limit_bytes=60 * 1024 * 1024
@@ -329,6 +376,7 @@
         backward.reshape((32,) + block),
         restrict_blocks.reshape((8,) + block),
     )
+    image, gathered = written(image, gathered)
     return image.reshape(source_field.shape), gathered.reshape((1, n_gz * n_gy) + field)
 
 

time: 49.7 us -> 53.4 us (1.074)
  Pallas kernels: 46.3 us -> 52.6 us
  local copies, waits for them, and re-layouts: 2.62 us -> 0 us
    pallas_call x1, Pallas kernels: 46.3 us -> 50.6 us  [per_device(): pl.pallas_call(functools.partial(kernel, sizes), out_shape=(jax.ShapeDtyp...]
    unnamed x4 -> x0, local copies, waits for them, and re-layouts: 2.62 us -> none
    pallas_call x0 -> x1, Pallas kernels: none -> 2 us  [written(): pl.pallas_call(write, out_shape=(jax.ShapeDtypeStruct(image.shape, image....]
where the time goes in v4:
time: 53.4 us; the launch traced here: 53.2 us
  Pallas kernels  52.6 us (99%)
  between operations  0.64 us (1%)
    pallas_call x1, Pallas kernels, per_device(): pl.pallas_call(functools.partial(kernel, sizes), out_shape=(jax.ShapeDtyp...  50.6 us
    pallas_call x1, Pallas kernels, written(): pl.pallas_call(write, out_shape=(jax.ShapeDtypeStruct(image.shape, image....  2 us

profile of v4, /device:TPU:0, one launch (start us, length us, event | category | flops | bytes accessed | tf_op | source)
XLA Modules:
  0.0 53.2 jit_solution(6628133080577678544)
XLA Ops:
  0.6 50.6 %shard_map.68 = (bf16[8,256,128]{2,1,0:T(8,128)(2,1)}, bf16[4,256,128]{2,1,0:T(8,128)(2,1)}) custom-call(bf16[8,256,128]{2,1,0:T(8,128)(2,1)} %bitcast.9, bf16[8,128,128]{2,1,0:T(8,128)(2,1)} %bitcast.10, bf16[32,128,128]{2,1,0:T(8,128)(2,1)} %bitcast.7, bf16[32,128,128]{2,1,0:T(8,128)(2,1)} %bitcast.8, bf16[8,128,128]{2,1,0:T(8,128)(2,1)} %bitcast.11), custom_call_target="tpu_custom_call" | custom-call | tf_op jit(solution)/shard_map/pallas_call | solution.py:341
  51.2 2.0 %shard_map.69 = (bf16[8,256,128]{2,1,0:T(8,128)(2,1)}, bf16[4,256,128]{2,1,0:T(8,128)(2,1)}) custom-call(bf16[8,256,128]{2,1,0:T(8,128)(2,1)} %get-tuple-element.6.image, bf16[4,256,128]{2,1,0:T(8,128)(2,1)} %get-tuple-element.7.gathered), custom_call_target="tpu_custom_call" | custom-call | tf_op jit(solution)/shard_map/pallas_call | solution.py:316

commit v5 on v3

--- a/solution.py
+++ b/solution.py
@@ -8,10 +8,10 @@
 from jax.sharding import PartitionSpec as P
 
 MESH = pl.DeviceIdType.MESH
-LAG = 5
-AHEAD = 6
-Z_AHEAD = 8
-PARTS = 2
+LAG = 2
+AHEAD = 3
+Z_AHEAD = 4
+PARTS = 1
 IMAGE = 8 * PARTS
 UNITS = 2 * IMAGE
 
@@ -73,8 +73,8 @@
     rows = src.shape[1] // PARTS
 
     def split(u):
-        part = lax.rem(u // 8, PARTS)
-        return u // IMAGE, pl.ds(pl.multiple_of(part * rows, rows), rows), lax.rem(u, 8)
+        part = u // 8 % PARTS
+        return u // IMAGE, pl.ds(part * rows, rows), u % 8
 
     def near(u, source):
         img, r, s = split(u)
@@ -105,13 +105,13 @@
 
     def y_vector(u):
         img, r, s = split(u)
-        k = 2 * (s // 4) + lax.rem(s, 2)
+        k = 2 * (s // 4) + s % 2
         return remote(V.at[img * 16 + s, r], V.at[img * 16 + 12 + k, r], y_send.at[u],
                       y_recv.at[u + 2], (ta, gz, y_down))
 
     def y_formed(u):
         img, r, s = split(u)
-        k = 2 * (s // 4) + lax.rem(s, 2)
+        k = 2 * (s // 4) + s % 2
         return remote(PY.at[img * 12 + s, r], PY.at[img * 12 + 8 + k, r], y_send.at[u],
                       y_recv.at[u - 2], (ta, gz, y_up))
 
@@ -122,28 +122,23 @@
     def send_time(u, source):
         near(u, source).start()
 
-        @pl.when(u < 8)
-        def _():
-            block0(lax.rem(u, 8)).start()
+        if u < 8:
+            block0(u % 8).start()
 
     def send_z(target):
-        @pl.when(lax.rem(target, 8) < 4)
-        def _():
+        if target % 8 < 4:
             z_formed(target + 4).start()
 
-        @pl.when(lax.rem(target, 8) >= 4)
-        def _():
+        if target % 8 >= 4:
             z_vector(target - 4).start()
 
     def send_y(u):
-        y = lax.rem(u // 2, 2)
-
-        @pl.when(y == 0)
-        def _():
+        y = (u // 2) % 2
+
+        if y == 0:
             y_vector(u).start()
 
-        @pl.when(y == 1)
-        def _():
+        if y == 1:
             y_formed(u).start()
 
     def form(img, r, s, vector):
@@ -154,31 +149,26 @@
         PY[img * 12 + s, r] = formed[:, width : 2 * width]
         PX[img * 8 + s, r] = formed[:, 2 * width :]
 
-    @pl.loop(0, AHEAD)
-    def _(u):
-        send_time(u, src.at[lax.rem(u, 8)])
+    for u in range(0, AHEAD):
+        send_time(u, src.at[u % 8])
 
     fetch[0].wait()
     fetch[1].wait()
 
-    @pl.loop(0, 8)
-    def _(index):
-        s = lax.rem(index + 4, 8)
+    for index in range(0, 8):
+        s = (index + 4) % 8
         everything = pl.ds(0, PARTS * rows)
         form(0, everything, s, V[s])
 
-        @pl.when(index < 4)
-        def _():
+        if index < 4:
             send_z(index)
 
         send_y(s)
 
-    @pl.loop(4, Z_AHEAD)
-    def _(u):
+    for u in range(4, Z_AHEAD):
         send_z(u)
 
-    @pl.loop(8, IMAGE)
-    def _(u):
+    for u in range(8, IMAGE):
         send_y(u)
 
     for copy in fetch[2:]:
@@ -188,7 +178,7 @@
     place = gz * n_gy + gy
 
     def gather(part):
-        r = pl.ds(pl.multiple_of(part * rows, rows), rows)
+        r = pl.ds(part * rows, rows)
         copies = [pltpu.make_async_copy(own_r.at[r], gathered.at[place, r], g_local.at[part])]
         for index, (a, b) in enumerate(others):
             oz, oy = other(a, b)
@@ -202,15 +192,14 @@
 
     def finish(u):
         img, r, s = split(u)
-        z, y, x = s // 4, lax.rem(s // 2, 2), lax.rem(s, 2)
+        z, y, x = s // 4, (s // 2) % 2, s % 2
         k = 2 * z + x
         base = img * 16
         y_next = base + (1 - y) * (s + 2) + y * (12 + k)
         y_from = img * 12 + y * (s - 2) + (1 - y) * (8 + k)
         flip = s + 1 - 2 * x
 
-        @pl.when(u < 8)
-        def _():
+        if u < 8:
             block0(s).wait_recv()
 
         z_any(u).wait_recv()
@@ -225,63 +214,84 @@
             total = total + formed.astype(jnp.float32)
         value = total.astype(jnp.bfloat16)
 
-        @pl.when(u < IMAGE)
-        def _():
+        if u < IMAGE:
             V[16 + s, r] = value
             form(1, r, s, value)
             send_y(u + IMAGE)
 
-        @pl.when(u >= IMAGE)
-        def _():
+        if u >= IMAGE:
             O[s, r] = value
             result(u).start()
             total_r[r] += times(value, R[s])
 
-            @pl.when(s == 7)
-            def _():
+            if s == 7:
                 own_r[r] = total_r[r].astype(jnp.bfloat16)
-                for copy in gather(lax.rem(u // 8, PARTS)):
+                for copy in gather(u // 8 % PARTS):
                     copy.start()
 
-        @pl.when(u + Z_AHEAD < UNITS)
-        def _():
+        if u + Z_AHEAD < UNITS:
             send_z(u + Z_AHEAD)
 
-    @pl.loop(0, UNITS + LAG)
-    def _(u):
-        @pl.when(u < UNITS)
-        def _():
+    for u in range(0, UNITS + LAG):
+        if u < UNITS:
             near(u, V.at[0]).wait_recv()
             far(u).start()
 
-        @pl.when(u + AHEAD < UNITS)
-        def _():
+        if u + AHEAD < UNITS:
             v = u + AHEAD
-            send_time(v, V.at[v // IMAGE * 16 + lax.rem(v, 8)])
-
-        @pl.when(u >= LAG)
-        def _():
+            send_time(v, V.at[v // IMAGE * 16 + v % 8])
+
+        if u >= LAG:
             finish(u - LAG)
 
-    @pl.loop(0, UNITS)
-    def _(u):
+    for u in range(0, UNITS):
         near(u, V.at[0]).wait_send()
         far(u).wait_send()
         z_any(u).wait_send()
         y_any(u).wait_send()
 
-    @pl.loop(0, 8)
-    def _(s):
+    for s in range(0, 8):
         block0(s).wait_send()
 
-    @pl.loop(IMAGE, UNITS)
-    def _(u):
+    for u in range(IMAGE, UNITS):
         result(u).wait()
 
-    @pl.loop(0, PARTS)
-    def _(part):
+    for part in range(0, PARTS):
         for copy in gather(part):
             copy.wait()
+
+
+def write(image, gathered, image_out, gathered_out, held, inward, outward):
+    parts = [(image.at[s], image_out.at[s]) for s in range(image.shape[0])]
+    parts += [(gathered.at[s], gathered_out.at[s]) for s in range(gathered.shape[0])]
+    reads = [pltpu.make_async_copy(a, held.at[i], inward.at[i]) for i, (a, _) in enumerate(parts)]
+    writes = [pltpu.make_async_copy(held.at[i], b, outward.at[i]) for i, (_, b) in enumerate(parts)]
+    for copy in reads:
+        copy.start()
+    for read, copy in zip(reads, writes):
+        read.wait()
+        copy.start()
+    for copy in writes:
+        copy.wait()
+
+
+def written(image, gathered):
+    count = image.shape[0] + gathered.shape[0]
+    return pl.pallas_call(
+        write,
+        out_shape=(
+            jax.ShapeDtypeStruct(image.shape, image.dtype),
+            jax.ShapeDtypeStruct(gathered.shape, gathered.dtype),
+        ),
+        in_specs=[pl.BlockSpec(memory_space=pltpu.HBM)] * 2,
+        out_specs=(pl.BlockSpec(memory_space=pltpu.HBM), pl.BlockSpec(memory_space=pltpu.HBM)),
+        scratch_shapes=[
+            pltpu.VMEM((count,) + image.shape[1:], image.dtype),
+            pltpu.SemaphoreType.DMA((count,)),
+            pltpu.SemaphoreType.DMA((count,)),
+        ],
+        compiler_params=pltpu.CompilerParams(vmem_limit_bytes=60 * 1024 * 1024),
+    )(image, gathered)
 
 
 def per_device(sizes, source_field, clover, forward, backward, restrict_blocks):
@@ -329,6 +339,7 @@
         backward.reshape((32,) + block),
         restrict_blocks.reshape((8,) + block),
     )
+    image, gathered = written(image, gathered)
     return image.reshape(source_field.shape), gathered.reshape((1, n_gz * n_gy) + field)
 
 

time: 49.7 us -> 49.6 us (level)
  local copies, waits for them, and re-layouts: 2.62 us -> 0 us
  Pallas kernels: 46.3 us -> 48.7 us
    unnamed x4 -> x0, local copies, waits for them, and re-layouts: 2.62 us -> none
    pallas_call x0 -> x1, Pallas kernels: none -> 2 us  [written(): pl.pallas_call(write, out_shape=(jax.ShapeDtypeStruct(image.shape, image....]
where the time goes in v5:
time: 49.6 us; the launch traced here: 49.4 us
  Pallas kernels  48.7 us (98%)
  between operations  0.64 us (1%)
    pallas_call x1, Pallas kernels, per_device(): pl.pallas_call(functools.partial(kernel, sizes), out_shape=(jax.ShapeDtyp...  46.7 us
    pallas_call x1, Pallas kernels, written(): pl.pallas_call(write, out_shape=(jax.ShapeDtypeStruct(image.shape, image....  2 us

profile of v5, /device:TPU:0, one launch (start us, length us, event | category | flops | bytes accessed | tf_op | source)
XLA Modules:
  0.0 49.4 jit_solution(18186437164219212905)
XLA Ops:
  0.6 46.7 %shard_map.68 = (bf16[8,256,128]{2,1,0:T(8,128)(2,1)}, bf16[4,256,128]{2,1,0:T(8,128)(2,1)}) custom-call(bf16[8,256,128]{2,1,0:T(8,128)(2,1)} %bitcast.9, bf16[8,128,128]{2,1,0:T(8,128)(2,1)} %bitcast.10, bf16[32,128,128]{2,1,0:T(8,128)(2,1)} %bitcast.7, bf16[32,128,128]{2,1,0:T(8,128)(2,1)} %bitcast.8, bf16[8,128,128]{2,1,0:T(8,128)(2,1)} %bitcast.11), custom_call_target="tpu_custom_call" | custom-call | tf_op jit(solution)/shard_map/pallas_call | solution.py:305
  47.4 2.0 %shard_map.69 = (bf16[8,256,128]{2,1,0:T(8,128)(2,1)}, bf16[4,256,128]{2,1,0:T(8,128)(2,1)}) custom-call(bf16[8,256,128]{2,1,0:T(8,128)(2,1)} %get-tuple-element.6.image, bf16[4,256,128]{2,1,0:T(8,128)(2,1)} %get-tuple-element.7.gathered), custom_call_target="tpu_custom_call" | custom-call | tf_op jit(solution)/shard_map/pallas_call | solution.py:280

commit v6 on v4

--- a/solution.py
+++ b/solution.py
@@ -26,7 +26,7 @@
     sizes,
     src, clo, fwd, bwd, res,
     image, gathered,
-    V, T, PZ, PY, PX, TB, C, F, B, R, O, early, total_r, own_r,
+    V, T, PZ, PY, PX, B0, C, F, B, R, O, total_r, own_r,
     near_send, near_recv, far_send, far_recv, b0_send, b0_recv,
     z_send, z_recv, y_send, y_recv, local, out_sem, g_send, g_recv, g_local,
 ):
@@ -35,17 +35,15 @@
     odd = lax.rem(ta, 2)
     partner = ta + 1 - 2 * odd
     beyond = lax.rem(ta + 2 - 4 * odd + n_ta, n_ta)
-    following = lax.rem(ta + 1, n_ta)
     z_up, z_down = lax.rem(gz + 1, n_gz), lax.rem(gz + n_gz - 1, n_gz)
     y_up, y_down = lax.rem(gy + 1, n_gy), lax.rem(gy + n_gy - 1, n_gy)
 
     fetch = [
         pltpu.make_async_copy(src, V.at[pl.ds(0, 8)], local.at[0]),
         pltpu.make_async_copy(bwd.at[pl.ds(8, 24)], B, local.at[1]),
-        pltpu.make_async_copy(fwd.at[pl.ds(8, 24)], F, local.at[2]),
+        pltpu.make_async_copy(fwd, F, local.at[2]),
         pltpu.make_async_copy(clo, C, local.at[3]),
         pltpu.make_async_copy(res, R, local.at[4]),
-        pltpu.make_async_copy(fwd.at[pl.ds(0, 8)], TB.at[0], local.at[5]),
     ]
     for copy in fetch:
         copy.start()
@@ -56,14 +54,12 @@
         return lax.rem(gz + a, n_gz), lax.rem(gz * 0 + gy + b, n_gy)
 
     barrier = pltpu.get_barrier_semaphore()
-    for step in (1, 2, n_ta - 1, n_ta - 2):
-        pl.semaphore_signal(
-            barrier, inc=1, device_id=(lax.rem(ta + step, n_ta), gz, gy), device_id_type=MESH
-        )
+    for neighbour in (partner, lax.rem(ta + 2, n_ta), lax.rem(ta + n_ta - 2, n_ta)):
+        pl.semaphore_signal(barrier, inc=1, device_id=(neighbour, gz, gy), device_id_type=MESH)
     for a, b in others:
         oz, oy = other(a, b)
         pl.semaphore_signal(barrier, inc=1, device_id=(ta, oz, oy), device_id_type=MESH)
-    pl.semaphore_wait(barrier, 4 + len(others))
+    pl.semaphore_wait(barrier, 3 + len(others))
 
     def remote(source, target, send, recv, device):
         return pltpu.make_async_remote_copy(
@@ -79,16 +75,16 @@
 
     def near(u, source):
         img, r, s = split(u)
-        return remote(source.at[r], T.at[img, 1 - odd, s, r], near_send.at[u], near_recv.at[u],
+        return remote(source.at[r], T.at[img, 0, s, r], near_send.at[u], near_recv.at[u],
                       (partner, gz, gy))
 
     def far(u):
         img, r, s = split(u)
-        return remote(T.at[img, odd, s, r], T.at[img, 1 - odd, s, r], far_send.at[u],
+        return remote(T.at[img, 2 - 2 * odd, s, r], T.at[img, 1, s, r], far_send.at[u],
                       far_recv.at[u], (beyond, gz, gy))
 
     def block0(s):
-        return remote(bwd.at[s], TB.at[1, s], b0_send.at[s], b0_recv.at[s], (following, gz, gy))
+        return remote(bwd.at[s], B0.at[s], b0_send.at[s], b0_recv.at[s], (partner, gz, gy))
 
     def z_vector(u):
         img, r, s = split(u)
@@ -121,11 +117,11 @@
                       y_recv.at[u], (ta, gz, y_up))
 
     def send_time(u, source):
+        @pl.when(u < 8)
+        def _():
+            block0(lax.rem(u, 8)).start()
+
         near(u, source).start()
-
-        @pl.when(u < 8)
-        def _():
-            block0(lax.rem(u, 8)).start()
 
     def send_z(target):
         @pl.when(lax.rem(target, 8) < 4)
@@ -201,11 +197,7 @@
         img, r, s = split(u)
         return pltpu.make_async_copy(O.at[s, r], image.at[s, r], out_sem.at[u - IMAGE])
 
-    def time_term(img, slot, s, r):
-        term = times(T[img, slot, s, r], TB[slot, s])
-        return jnp.where(slot == 1, term.astype(jnp.bfloat16).astype(jnp.float32), term)
-
-    def begin(u):
+    def finish(u):
         img, r, s = split(u)
         z, y, x = s // 4, lax.rem(s // 2, 2), lax.rem(s, 2)
         k = 2 * z + x
@@ -214,24 +206,16 @@
         y_from = img * 12 + y * (s - 2) + (1 - y) * (8 + k)
         flip = s + 1 - 2 * x
 
-        @pl.when(u < 8)
-        def _():
-            block0(s).wait_recv()
-
         z_any(u).wait_recv()
         y_any(u).wait_recv()
-        vectors = [V[base + s, r], V[base + flip, r], V[base + s + 4, r], V[y_next, r]]
-        blocks = [C[s], F[16 + s], F[s], F[8 + s]]
+        far(u).wait_recv()
+        vectors = [V[base + s, r], V[base + flip, r], V[base + s + 4, r], V[y_next, r],
+                   T[img, odd, s, r]]
+        blocks = [C[s], F[24 + s], F[8 + s], F[16 + s], F[s]]
         total = times(jnp.concatenate(vectors, axis=1), jnp.concatenate(blocks, axis=1))
-        total = total + time_term(img, odd, s, r)
-        for formed in (PX[img * 8 + flip, r], PZ[img * 12 + s, r], PY[y_from, r]):
+        for formed in (PX[img * 8 + flip, r], PZ[img * 12 + s, r], PY[y_from, r],
+                       T[img, 1 + odd, s, r]):
             total = total + formed.astype(jnp.float32)
-        early[lax.rem(u, 8)] = total
-
-    def finish(u):
-        img, r, s = split(u)
-        far(u).wait_recv()
-        total = early[lax.rem(u, 8)] + time_term(img, 1 - odd, s, r)
         value = total.astype(jnp.bfloat16)
 
         @pl.when(u < IMAGE)
@@ -260,17 +244,20 @@
     def _(u):
         @pl.when(u < UNITS)
         def _():
+            img, r, s = split(u)
             near(u, V.at[0]).wait_recv()
+
+            @pl.when(u < 8)
+            def _():
+                block0(s).wait_recv()
+
+            T[img, 2, s, r] = times(T[img, 0, s, r], B0[s]).astype(jnp.bfloat16)
             far(u).start()
 
         @pl.when(u + AHEAD < UNITS)
         def _():
             v = u + AHEAD
             send_time(v, V.at[v // IMAGE * 16 + lax.rem(v, 8)])
-
-        @pl.when(u < UNITS)
-        def _():
-            begin(u)
 
         @pl.when(u >= LAG)
         def _():
@@ -348,23 +335,22 @@
         out_specs=(pl.BlockSpec(memory_space=pltpu.HBM), pl.BlockSpec(memory_space=pltpu.HBM)),
         scratch_shapes=[
             pltpu.VMEM((32,) + field, bf16),
-            pltpu.VMEM((2, 2, 8) + field, bf16),
+            pltpu.VMEM((2, 3, 8) + field, bf16),
             pltpu.VMEM((24,) + field, bf16),
             pltpu.VMEM((24,) + field, bf16),
             pltpu.VMEM((16,) + field, bf16),
-            pltpu.VMEM((2, 8) + block, bf16),
             pltpu.VMEM((8,) + block, bf16),
-            pltpu.VMEM((24,) + block, bf16),
+            pltpu.VMEM((8,) + block, bf16),
+            pltpu.VMEM((32,) + block, bf16),
             pltpu.VMEM((24,) + block, bf16),
             pltpu.VMEM((8,) + block, bf16),
             pltpu.VMEM((8,) + field, bf16),
-            pltpu.VMEM((8, rows // PARTS, width), jnp.float32),
             pltpu.VMEM(field, jnp.float32),
             pltpu.VMEM(field, bf16),
             dma((UNITS,)), dma((UNITS,)), dma((UNITS,)), dma((UNITS,)),
             dma((8,)), dma((8,)),
             dma((UNITS,)), dma((UNITS,)), dma((UNITS,)), dma((UNITS,)),
-            dma((6,)), dma((IMAGE,)), dma((PARTS, others)), dma((PARTS, others)), dma((PARTS,)),
+            dma((5,)), dma((IMAGE,)), dma((PARTS, others)), dma((PARTS, others)), dma((PARTS,)),
         ],
         compiler_params=pltpu.CompilerParams(
             collective_id=0, has_side_effects=True, vmem_limit_bytes=60 * 1024 * 1024

time: 53.4 us -> 50.4 us (0.944)
  Pallas kernels: 52.6 us -> 49.5 us
    pallas_call x1, Pallas kernels: 50.6 us -> 47.5 us  [per_device(): pl.pallas_call(functools.partial(kernel, sizes), out_shape=(jax.ShapeDtyp...]
where the time goes in v6:
time: 50.4 us; the launch traced here: 50.2 us
  Pallas kernels  49.5 us (98%)
  between operations  0.64 us (1%)
    pallas_call x1, Pallas kernels, per_device(): pl.pallas_call(functools.partial(kernel, sizes), out_shape=(jax.ShapeDtyp...  47.5 us
    pallas_call x1, Pallas kernels, written(): pl.pallas_call(write, out_shape=(jax.ShapeDtypeStruct(image.shape, image....  2 us

profile of v6, /device:TPU:0, one launch (start us, length us, event | category | flops | bytes accessed | tf_op | source)
XLA Modules:
  0.0 50.2 jit_solution(11514811426157370302)
XLA Ops:
  0.6 47.5 %shard_map.68 = (bf16[8,256,128]{2,1,0:T(8,128)(2,1)}, bf16[4,256,128]{2,1,0:T(8,128)(2,1)}) custom-call(bf16[8,256,128]{2,1,0:T(8,128)(2,1)} %bitcast.9, bf16[8,128,128]{2,1,0:T(8,128)(2,1)} %bitcast.10, bf16[32,128,128]{2,1,0:T(8,128)(2,1)} %bitcast.7, bf16[32,128,128]{2,1,0:T(8,128)(2,1)} %bitcast.8, bf16[8,128,128]{2,1,0:T(8,128)(2,1)} %bitcast.11), custom_call_target="tpu_custom_call" | custom-call | tf_op jit(solution)/shard_map/pallas_call | solution.py:328
  48.2 2.0 %shard_map.69 = (bf16[8,256,128]{2,1,0:T(8,128)(2,1)}, bf16[4,256,128]{2,1,0:T(8,128)(2,1)}) custom-call(bf16[8,256,128]{2,1,0:T(8,128)(2,1)} %get-tuple-element.6.image, bf16[4,256,128]{2,1,0:T(8,128)(2,1)} %get-tuple-element.7.gathered), custom_call_target="tpu_custom_call" | custom-call | tf_op jit(solution)/shard_map/pallas_call | solution.py:303

commit v7 on v5

--- a/solution.py
+++ b/solution.py
@@ -11,9 +11,8 @@
 LAG = 2
 AHEAD = 3
 Z_AHEAD = 4
-PARTS = 1
-IMAGE = 8 * PARTS
-UNITS = 2 * IMAGE
+UNITS = 16
+PIECES = 17
 
 
 def times(vector, block):
@@ -35,7 +34,6 @@
     odd = lax.rem(ta, 2)
     partner = ta + 1 - 2 * odd
     beyond = lax.rem(ta + 2 - 4 * odd + n_ta, n_ta)
-    following = lax.rem(ta + 1, n_ta)
     z_up, z_down = lax.rem(gz + 1, n_gz), lax.rem(gz + n_gz - 1, n_gz)
     y_up, y_down = lax.rem(gy + 1, n_gy), lax.rem(gy + n_gy - 1, n_gy)
 
@@ -55,14 +53,12 @@
         return lax.rem(gz + a, n_gz), lax.rem(gz * 0 + gy + b, n_gy)
 
     barrier = pltpu.get_barrier_semaphore()
-    for step in (1, 2, n_ta - 1, n_ta - 2):
-        pl.semaphore_signal(
-            barrier, inc=1, device_id=(lax.rem(ta + step, n_ta), gz, gy), device_id_type=MESH
-        )
+    for neighbour in (partner, lax.rem(ta + 2, n_ta), lax.rem(ta + n_ta - 2, n_ta)):
+        pl.semaphore_signal(barrier, inc=1, device_id=(neighbour, gz, gy), device_id_type=MESH)
     for a, b in others:
         oz, oy = other(a, b)
         pl.semaphore_signal(barrier, inc=1, device_id=(ta, oz, oy), device_id_type=MESH)
-    pl.semaphore_wait(barrier, 4 + len(others))
+    pl.semaphore_wait(barrier, 3 + len(others))
 
     def remote(source, target, send, recv, device):
         return pltpu.make_async_remote_copy(
@@ -70,24 +66,29 @@
             device_id=device, device_id_type=MESH,
         )
 
-    rows = src.shape[1] // PARTS
+    rows = src.shape[1]
+    half = rows // 2
 
     def split(u):
-        part = u // 8 % PARTS
-        return u // IMAGE, pl.ds(part * rows, rows), u % 8
-
-    def near(u, source):
-        img, r, s = split(u)
-        return remote(source.at[r], T.at[img, 1 - odd, s, r], near_send.at[u], near_recv.at[u],
+        return u // 8, pl.ds(0, rows), u % 8
+
+    def piece(q):
+        if q < UNITS - 1:
+            return q // 8, pl.ds(0, rows), q % 8
+        return 1, pl.ds((q - UNITS + 1) * half, half), 7
+
+    def near(q, source):
+        img, r, s = piece(q)
+        return remote(source.at[r], T.at[img, 0, s, r], near_send.at[q], near_recv.at[q],
                       (partner, gz, gy))
 
-    def far(u):
-        img, r, s = split(u)
-        return remote(T.at[img, odd, s, r], T.at[img, 1 - odd, s, r], far_send.at[u],
-                      far_recv.at[u], (beyond, gz, gy))
+    def far(q):
+        img, r, s = piece(q)
+        return remote(T.at[img, 2 - 2 * odd, s, r], T.at[img, 1, s, r], far_send.at[q],
+                      far_recv.at[q], (beyond, gz, gy))
 
     def block0(s):
-        return remote(bwd.at[s], B0.at[s], b0_send.at[s], b0_recv.at[s], (following, gz, gy))
+        return remote(bwd.at[s], B0.at[s], b0_send.at[s], b0_recv.at[s], (partner, gz, gy))
 
     def z_vector(u):
         img, r, s = split(u)
@@ -120,10 +121,10 @@
                       y_recv.at[u], (ta, gz, y_up))
 
     def send_time(u, source):
-        near(u, source).start()
-
         if u < 8:
             block0(u % 8).start()
+
+        near(u, source).start()
 
     def send_z(target):
         if target % 8 < 4:
@@ -157,19 +158,13 @@
 
     for index in range(0, 8):
         s = (index + 4) % 8
-        everything = pl.ds(0, PARTS * rows)
+        everything = pl.ds(0, rows)
         form(0, everything, s, V[s])
 
         if index < 4:
             send_z(index)
 
         send_y(s)
-
-    for u in range(4, Z_AHEAD):
-        send_z(u)
-
-    for u in range(8, IMAGE):
-        send_y(u)
 
     for copy in fetch[2:]:
         copy.wait()
@@ -178,7 +173,7 @@
     place = gz * n_gy + gy
 
     def gather(part):
-        r = pl.ds(part * rows, rows)
+        r = pl.ds(part * half, half)
         copies = [pltpu.make_async_copy(own_r.at[r], gathered.at[place, r], g_local.at[part])]
         for index, (a, b) in enumerate(others):
             oz, oy = other(a, b)
@@ -186,12 +181,13 @@
                                  g_recv.at[part, index], (ta, oz, oy)))
         return copies
 
-    def result(u):
-        img, r, s = split(u)
-        return pltpu.make_async_copy(O.at[s, r], image.at[s, r], out_sem.at[u - IMAGE])
-
-    def finish(u):
-        img, r, s = split(u)
+    def result(q):
+        img, r, s = piece(q)
+        return pltpu.make_async_copy(O.at[s, r], image.at[s, r], out_sem.at[q - 8])
+
+    def finish(q):
+        img, r, s = piece(q)
+        u = img * 8 + s
         z, y, x = s // 4, (s // 2) % 2, s % 2
         k = 2 * z + x
         base = img * 16
@@ -199,64 +195,69 @@
         y_from = img * 12 + y * (s - 2) + (1 - y) * (8 + k)
         flip = s + 1 - 2 * x
 
-        if u < 8:
-            block0(s).wait_recv()
-
-        z_any(u).wait_recv()
-        y_any(u).wait_recv()
-        far(u).wait_recv()
+        if q == u:
+            z_any(u).wait_recv()
+            y_any(u).wait_recv()
+        far(q).wait_recv()
         vectors = [V[base + s, r], V[base + flip, r], V[base + s + 4, r], V[y_next, r],
-                   T[img, 0, s, r]]
+                   T[img, odd, s, r]]
         blocks = [C[s], F[24 + s], F[8 + s], F[16 + s], F[s]]
         total = times(jnp.concatenate(vectors, axis=1), jnp.concatenate(blocks, axis=1))
         for formed in (PX[img * 8 + flip, r], PZ[img * 12 + s, r], PY[y_from, r],
-                       times(T[img, 1, s, r], B0[s]).astype(jnp.bfloat16)):
+                       T[img, 1 + odd, s, r]):
             total = total + formed.astype(jnp.float32)
         value = total.astype(jnp.bfloat16)
 
-        if u < IMAGE:
+        if img == 0:
             V[16 + s, r] = value
             form(1, r, s, value)
-            send_y(u + IMAGE)
-
-        if u >= IMAGE:
+            send_y(u + 8)
+        else:
             O[s, r] = value
-            result(u).start()
+            result(q).start()
             total_r[r] += times(value, R[s])
 
             if s == 7:
                 own_r[r] = total_r[r].astype(jnp.bfloat16)
-                for copy in gather(u // 8 % PARTS):
+                for copy in gather(q - UNITS + 1):
                     copy.start()
 
         if u + Z_AHEAD < UNITS:
             send_z(u + Z_AHEAD)
 
-    for u in range(0, UNITS + LAG):
-        if u < UNITS:
-            near(u, V.at[0]).wait_recv()
-            far(u).start()
-
-        if u + AHEAD < UNITS:
-            v = u + AHEAD
-            send_time(v, V.at[v // IMAGE * 16 + v % 8])
-
-        if u >= LAG:
-            finish(u - LAG)
-
-    for u in range(0, UNITS):
-        near(u, V.at[0]).wait_send()
-        far(u).wait_send()
+    for q in range(PIECES + LAG):
+        if q < PIECES:
+            img, r, s = piece(q)
+            near(q, V.at[0]).wait_recv()
+
+            if q < 8:
+                block0(s).wait_recv()
+
+            T[img, 2, s, r] = times(T[img, 0, s, r], B0[s]).astype(jnp.bfloat16)
+            far(q).start()
+
+        if q + AHEAD < PIECES:
+            later, _, site = piece(q + AHEAD)
+            send_time(q + AHEAD, V.at[later * 16 + site])
+
+        if q >= LAG:
+            finish(q - LAG)
+
+    for u in range(UNITS):
         z_any(u).wait_send()
         y_any(u).wait_send()
 
-    for s in range(0, 8):
+    for q in range(PIECES):
+        near(q, V.at[0]).wait_send()
+        far(q).wait_send()
+
+    for s in range(8):
         block0(s).wait_send()
 
-    for u in range(IMAGE, UNITS):
-        result(u).wait()
-
-    for part in range(0, PARTS):
+    for q in range(8, PIECES):
+        result(q).wait()
+
+    for part in range(2):
         for copy in gather(part):
             copy.wait()
 
@@ -312,7 +313,7 @@
         out_specs=(pl.BlockSpec(memory_space=pltpu.HBM), pl.BlockSpec(memory_space=pltpu.HBM)),
         scratch_shapes=[
             pltpu.VMEM((32,) + field, bf16),
-            pltpu.VMEM((2, 2, 8) + field, bf16),
+            pltpu.VMEM((2, 3, 8) + field, bf16),
             pltpu.VMEM((24,) + field, bf16),
             pltpu.VMEM((24,) + field, bf16),
             pltpu.VMEM((16,) + field, bf16),
@@ -324,10 +325,10 @@
             pltpu.VMEM((8,) + field, bf16),
             pltpu.VMEM(field, jnp.float32),
             pltpu.VMEM(field, bf16),
-            dma((UNITS,)), dma((UNITS,)), dma((UNITS,)), dma((UNITS,)),
+            dma((PIECES,)), dma((PIECES,)), dma((PIECES,)), dma((PIECES,)),
             dma((8,)), dma((8,)),
             dma((UNITS,)), dma((UNITS,)), dma((UNITS,)), dma((UNITS,)),
-            dma((5,)), dma((IMAGE,)), dma((PARTS, others)), dma((PARTS, others)), dma((PARTS,)),
+            dma((5,)), dma((PIECES - 8,)), dma((2, others)), dma((2, others)), dma((2,)),
         ],
         compiler_params=pltpu.CompilerParams(
             collective_id=0, has_side_effects=True, vmem_limit_bytes=60 * 1024 * 1024

time: 49.6 us -> 49.9 us (level)
  no operation moved by 1% of the time
where the time goes in v7:
time: 49.9 us; the launch traced here: 49.7 us
  Pallas kernels  49.1 us (98%)
  between operations  0.64 us (1%)
    pallas_call x1, Pallas kernels, per_device(): pl.pallas_call(functools.partial(kernel, sizes), out_shape=(jax.ShapeDtyp...  47.1 us
    pallas_call x1, Pallas kernels, written(): pl.pallas_call(write, out_shape=(jax.ShapeDtypeStruct(image.shape, image....  2 us

profile of v7, /device:TPU:0, one launch (start us, length us, event | category | flops | bytes accessed | tf_op | source)
XLA Modules:
  0.0 49.7 jit_solution(6426391668505977616)
XLA Ops:
  0.6 47.1 %shard_map.68 = (bf16[8,256,128]{2,1,0:T(8,128)(2,1)}, bf16[4,256,128]{2,1,0:T(8,128)(2,1)}) custom-call(bf16[8,256,128]{2,1,0:T(8,128)(2,1)} %bitcast.9, bf16[8,128,128]{2,1,0:T(8,128)(2,1)} %bitcast.10, bf16[32,128,128]{2,1,0:T(8,128)(2,1)} %bitcast.7, bf16[32,128,128]{2,1,0:T(8,128)(2,1)} %bitcast.8, bf16[8,128,128]{2,1,0:T(8,128)(2,1)} %bitcast.11), custom_call_target="tpu_custom_call" | custom-call | tf_op jit(solution)/shard_map/pallas_call | solution.py:306
  47.7 2.0 %shard_map.69 = (bf16[8,256,128]{2,1,0:T(8,128)(2,1)}, bf16[4,256,128]{2,1,0:T(8,128)(2,1)}) custom-call(bf16[8,256,128]{2,1,0:T(8,128)(2,1)} %get-tuple-element.6.image, bf16[4,256,128]{2,1,0:T(8,128)(2,1)} %get-tuple-element.7.gathered), custom_call_target="tpu_custom_call" | custom-call | tf_op jit(solution)/shard_map/pallas_call | solution.py:281

commit v8 on v7

--- a/solution.py
+++ b/solution.py
@@ -8,7 +8,7 @@
 from jax.sharding import PartitionSpec as P
 
 MESH = pl.DeviceIdType.MESH
-LAG = 2
+LAG = 4
 AHEAD = 3
 Z_AHEAD = 4
 UNITS = 16
@@ -225,7 +225,8 @@
         if u + Z_AHEAD < UNITS:
             send_z(u + Z_AHEAD)
 
-    for q in range(PIECES + LAG):
+    finished = 0
+    for q in range(PIECES + 1):
         if q < PIECES:
             img, r, s = piece(q)
             near(q, V.at[0]).wait_recv()
@@ -240,8 +241,11 @@
             later, _, site = piece(q + AHEAD)
             send_time(q + AHEAD, V.at[later * 16 + site])
 
-        if q >= LAG:
-            finish(q - LAG)
+        lag = LAG if q < UNITS - 3 else LAG - 1 if q < UNITS else LAG - 2
+        ready = q - lag if q < PIECES else PIECES - 1
+        while finished <= ready:
+            finish(finished)
+            finished += 1
 
     for u in range(UNITS):
         z_any(u).wait_send()

time: 49.9 us -> 48.4 us (0.970)
  Pallas kernels: 49.1 us -> 47.5 us
    pallas_call x1, Pallas kernels: 47.1 us -> 45.5 us  [per_device(): pl.pallas_call(functools.partial(kernel, sizes), out_shape=(jax.ShapeDtyp...]
where the time goes in v8:
time: 48.4 us; the launch traced here: 48.2 us
  Pallas kernels  47.5 us (98%)
  between operations  0.64 us (1%)
    pallas_call x1, Pallas kernels, per_device(): pl.pallas_call(functools.partial(kernel, sizes), out_shape=(jax.ShapeDtyp...  45.5 us
    pallas_call x1, Pallas kernels, written(): pl.pallas_call(write, out_shape=(jax.ShapeDtypeStruct(image.shape, image....  2 us

profile of v8, /device:TPU:0, one launch (start us, length us, event | category | flops | bytes accessed | tf_op | source)
XLA Modules:
  0.0 48.2 jit_solution(9041962837226411165)
XLA Ops:
  0.6 45.5 %shard_map.68 = (bf16[8,256,128]{2,1,0:T(8,128)(2,1)}, bf16[4,256,128]{2,1,0:T(8,128)(2,1)}) custom-call(bf16[8,256,128]{2,1,0:T(8,128)(2,1)} %bitcast.9, bf16[8,128,128]{2,1,0:T(8,128)(2,1)} %bitcast.10, bf16[32,128,128]{2,1,0:T(8,128)(2,1)} %bitcast.7, bf16[32,128,128]{2,1,0:T(8,128)(2,1)} %bitcast.8, bf16[8,128,128]{2,1,0:T(8,128)(2,1)} %bitcast.11), custom_call_target="tpu_custom_call" | custom-call | tf_op jit(solution)/shard_map/pallas_call | solution.py:310
  46.2 2.0 %shard_map.69 = (bf16[8,256,128]{2,1,0:T(8,128)(2,1)}, bf16[4,256,128]{2,1,0:T(8,128)(2,1)}) custom-call(bf16[8,256,128]{2,1,0:T(8,128)(2,1)} %get-tuple-element.6.image, bf16[4,256,128]{2,1,0:T(8,128)(2,1)} %get-tuple-element.7.gathered), custom_call_target="tpu_custom_call" | custom-call | tf_op jit(solution)/shard_map/pallas_call | solution.py:285

commit v9 on v8

--- a/solution.py
+++ b/solution.py
@@ -9,7 +9,6 @@
 
 MESH = pl.DeviceIdType.MESH
 LAG = 4
-AHEAD = 3
 Z_AHEAD = 4
 UNITS = 16
 PIECES = 17
@@ -150,7 +149,7 @@
         PY[img * 12 + s, r] = formed[:, width : 2 * width]
         PX[img * 8 + s, r] = formed[:, 2 * width :]
 
-    for u in range(0, AHEAD):
+    for u in range(8):
         send_time(u, src.at[u % 8])
 
     fetch[0].wait()
@@ -210,6 +209,8 @@
 
         if img == 0:
             V[16 + s, r] = value
+            for later in range(u + 8, PIECES if s == 7 else u + 9):
+                near(later, V.at[16 + s]).start()
             form(1, r, s, value)
             send_y(u + 8)
         else:
@@ -236,10 +237,6 @@
 
             T[img, 2, s, r] = times(T[img, 0, s, r], B0[s]).astype(jnp.bfloat16)
             far(q).start()
-
-        if q + AHEAD < PIECES:
-            later, _, site = piece(q + AHEAD)
-            send_time(q + AHEAD, V.at[later * 16 + site])
 
         lag = LAG if q < UNITS - 3 else LAG - 1 if q < UNITS else LAG - 2
         ready = q - lag if q < PIECES else PIECES - 1

time: 48.4 us -> 48.5 us (level)
  no operation moved by 1% of the time
where the time goes in v9:
time: 48.5 us; the launch traced here: 48.3 us
  Pallas kernels  47.7 us (98%)
  between operations  0.64 us (1%)
    pallas_call x1, Pallas kernels, per_device(): pl.pallas_call(functools.partial(kernel, sizes), out_shape=(jax.ShapeDtyp...  45.7 us
    pallas_call x1, Pallas kernels, written(): pl.pallas_call(write, out_shape=(jax.ShapeDtypeStruct(image.shape, image....  2 us

profile of v9, /device:TPU:0, one launch (start us, length us, event | category | flops | bytes accessed | tf_op | source)
XLA Modules:
  0.0 48.3 jit_solution(4922056532004143584)
XLA Ops:
  0.6 45.7 %shard_map.68 = (bf16[8,256,128]{2,1,0:T(8,128)(2,1)}, bf16[4,256,128]{2,1,0:T(8,128)(2,1)}) custom-call(bf16[8,256,128]{2,1,0:T(8,128)(2,1)} %bitcast.9, bf16[8,128,128]{2,1,0:T(8,128)(2,1)} %bitcast.10, bf16[32,128,128]{2,1,0:T(8,128)(2,1)} %bitcast.7, bf16[32,128,128]{2,1,0:T(8,128)(2,1)} %bitcast.8, bf16[8,128,128]{2,1,0:T(8,128)(2,1)} %bitcast.11), custom_call_target="tpu_custom_call" | custom-call | tf_op jit(solution)/shard_map/pallas_call | solution.py:307
  46.3 2.0 %shard_map.69 = (bf16[8,256,128]{2,1,0:T(8,128)(2,1)}, bf16[4,256,128]{2,1,0:T(8,128)(2,1)}) custom-call(bf16[8,256,128]{2,1,0:T(8,128)(2,1)} %get-tuple-element.6.image, bf16[4,256,128]{2,1,0:T(8,128)(2,1)} %get-tuple-element.7.gathered), custom_call_target="tpu_custom_call" | custom-call | tf_op jit(solution)/shard_map/pallas_call | solution.py:282
